TPU v7x, 32 devices: a whole 2x2x4 slice. The times are simulated.
32 devices in a mesh: groups: 2 (over y), gx: 8 (over z, x), gy: 2 (over core).
Axes of the slice: x: 2, y: 2, z: 4, core: 2. Of those that a mesh axis runs over, the one named last changes fastest.
Arguments:
- voxels: bfloat16 [16, 128, 128, 64], P(('groups', 'gx'), 'gy'), parts along dimension 0, may hold values from -6 to 6
- occupancy: int32 [16, 128, 128], P(('groups', 'gx'), 'gy'), parts along dimension 0, may hold values 0 or 1
- row_weights: bfloat16 [8, 64], P('gx'), may hold values from -2 to 2
- column_weights: bfloat16 [128, 64], P('gy'), may hold values from -0.5 to 0.5
- depth_weights: bfloat16 [128, 64], replicated, may hold values from -0.5 to 0.5
- plane_kernels: bfloat16 [3, 2, 3, 3, 64, 64], replicated, may hold values from -0.25 to 0.25
- expand_weight: bfloat16 [64, 128], replicated, may hold values from -0.75 to 0.75
- shrink_weight: bfloat16 [128, 64], replicated, may hold values from -1 to 1
Outputs:
- updated: bfloat16 [16, 128, 128, 64], P(('groups', 'gx'), 'gy'), parts along dimension 0
There are 2 independent parts, one for each index of `groups`. A program takes and returns all parts, laid end to end along the dimension named above; an argument that names none is the same for every part. Nothing has to cross between parts.
All inputs are finite; a program needn't handle non-finite values. No bound on the sum of `occupancy` on one device may be relied on, other than what follows from the above.
Results may differ from a plain program's by a relative error of at most 0.015.
Values may be sent and summed in bfloat16 or wider, within the bound.
No kernel may reach another device: no remote copies, remote signals or barrier semaphores. Data moves between devices by JAX's collectives and lax.ppermute only.
A program may use at most 64 MiB of HBM per device.

v0:
```python
import jax
import jax.numpy as jnp
from jax import lax
from jax.sharding import PartitionSpec as P

product_scale = 8.0


def with_halo(cells, sides, width):
    for axis, dim in sides:
        count = lax.axis_size(axis)
        ends = count - 1
        head = lax.slice_in_dim(cells, 0, width, axis=dim)
        tail = lax.slice_in_dim(cells, cells.shape[dim] - width, cells.shape[dim], axis=dim)
        cells = jnp.concatenate(
            [
                lax.ppermute(tail, axis, [(i, (i + 1) % count) for i in range(ends)]),
                cells,
                lax.ppermute(head, axis, [((i + 1) % count, i) for i in range(ends)]),
            ],
            axis=dim,
        )
    return cells


def conv_valid(padded, kernel):
    rows = padded.shape[0] - 2
    cols = padded.shape[1] - 2
    total = jnp.zeros((rows, cols, kernel.shape[-1]), jnp.float32)
    for row_off in range(3):
        for col_off in range(3):
            window = padded[row_off : row_off + rows, col_off : col_off + cols]
            total = total + jnp.einsum(
                "ijc,co->ijo", window, kernel[row_off, col_off], preferred_element_type=jnp.float32
            )
    return total


def plane_block(plane, kernels, extend):
    inner = jax.nn.silu(conv_valid(extend(plane), kernels[0])).astype(jnp.bfloat16)
    return conv_valid(extend(inner), kernels[1]).astype(jnp.bfloat16)


def rim_xy(plane):
    return with_halo(plane, (("gx", 0), ("gy", 1)), 1)


def rim_xz(plane):
    padded = with_halo(plane, (("gx", 0),), 1)
    return jnp.pad(padded, ((0, 0), (1, 1), (0, 0)))


def rim_yz(plane):
    padded = with_halo(plane, (("gy", 0),), 1)
    return jnp.pad(padded, ((0, 0), (1, 1), (0, 0)))


def shards(
    voxels,
    occupancy,
    row_weights,
    column_weights,
    depth_weights,
    plane_kernels,
    expand_weight,
    shrink_weight,
):
    features = voxels * occupancy.astype(jnp.bfloat16)[..., None]
    xy_plane = jnp.einsum(
        "xyzc,zc->xyc", features, depth_weights, preferred_element_type=jnp.float32
    ).astype(jnp.bfloat16)
    xz_part = jnp.einsum(
        "xyzc,yc->xzc", features, column_weights, preferred_element_type=jnp.float32
    )
    yz_part = jnp.einsum("xyzc,xc->yzc", features, row_weights, preferred_element_type=jnp.float32)
    xy_out = plane_block(xy_plane, plane_kernels[0], rim_xy)
    xz_plane = lax.psum(xz_part, "gy").astype(jnp.bfloat16)
    xz_out = plane_block(xz_plane, plane_kernels[1], rim_xz)
    yz_plane = lax.psum(yz_part, "gx").astype(jnp.bfloat16)
    yz_out = plane_block(yz_plane, plane_kernels[2], rim_yz)
    product = xy_out.astype(jnp.float32)[:, :, None, :] * xz_out.astype(jnp.float32)[:, None, :, :]
    product = product * yz_out.astype(jnp.float32)[None, :, :, :]
    mixed = (product_scale * product).astype(jnp.bfloat16)
    hidden = jax.nn.silu(
        jnp.einsum("xyzc,ch->xyzh", mixed, expand_weight, preferred_element_type=jnp.float32)
    ).astype(jnp.bfloat16)
    branch = jnp.einsum("xyzh,hc->xyzc", hidden, shrink_weight, preferred_element_type=jnp.float32)
    return (features.astype(jnp.float32) + branch).astype(jnp.bfloat16)


def solution(mesh):
    in_specs = (
        P(("groups", "gx"), "gy", None, None),
        P(("groups", "gx"), "gy", None),
        P("gx", None),
        P("gy", None),
        P(),
        P(),
        P(),
        P(),
    )
    out_specs = P(("groups", "gx"), "gy", None, None)
    return jax.shard_map(shards, mesh=mesh, in_specs=in_specs, out_specs=out_specs, check_vma=False)
```

profile of v0, /device:TPU:0, one launch (start us, length us, event | category | flops | bytes accessed | tf_op | source)
XLA Modules:
  0.0 184.1 jit_solution(3502592490292366999)
XLA Ops:
  1.4 1.7 convert_multiply_fusion
  5.2 5.5 %collective-permute-start = (bf16[1,64,64]{1,2,0:T(8,128)(2,1)S(1)}, bf16[1,64,64]{1,2,0:T(8,128)(2,1)S(1)}, u32[]{:S(2)}, u32[]{:S(2)}) collective-permute-start(bf16[1,64,64]{1,2,0:T(8,128)(2,1)S(1)} %convert_bitcast_fusion.1), channel_id=1, source_target_pairs={{0,2},{2,4},{4,6},{6,8},{8,10},{10,12},{12,14},{1,3},{3,5},{5,7},{... | collective-permute-start | bytes 24584 | tf_op jit(solution)/shard_map/ppermute | solution.py:17
  11.6 3.4 %psum.14 = bf16[1,128,64]{1,2,0:T(8,128)(2,1)S(1)} all-reduce(f32[1,128,64]{1,2,0:T(8,128)S(1)} %bitcast.374), channel_id=1, replica_groups=mesh['groups'=2,'gx'=8,'gy'=2] {'gy'}, use_global_device_ids=true, to_apply=%region_0.1 | all-reduce | flops 8192 | bytes 49152 | tf_op jit(solution)/shard_map/psum | solution.py:77
  16.3 6.1 %collective-permute-start.8 = (bf16[1,128,64]{1,2,0:T(8,128)(2,1)S(1)}, bf16[1,128,64]{1,2,0:T(8,128)(2,1)}, u32[]{:S(2)}, u32[]{:S(2)}) collective-permute-start(bf16[1,128,64]{1,2,0:T(8,128)(2,1)S(1)} %psum.14), channel_id=1, source_target_pairs={{0,2},{2,4},{4,6},{6,8},{8,10},{10,12},{12,14},{1,3},{3,5},{5,7},{... | collective-permute-start | bytes 49160 | tf_op jit(solution)/shard_map/ppermute | solution.py:17
  22.4 92.1 %all-reduce.5 = bf16[64,128,64]{1,2,0:T(8,128)(2,1)S(1)} all-reduce(f32[64,128,64]{1,2,0:T(8,128)S(1)} %get-tuple-element.5), channel_id=1, replica_groups=mesh['groups'=2,'gx'=8,'gy'=2] {'gx'}, use_global_device_ids=true, to_apply=%region_1.2 | all-reduce | flops 524288 | bytes 3145728 | tf_op jit(solution)/shard_map/psum | solution.py:79
  115.8 1.3 slice_bitcast_fusion.4
  118.5 1.3 collective-permute-start.2
  119.8 1.3 collective-permute-start.3
  126.2 1.3 collective-permute-start.5
  127.6 4.5 %collective-permute-start.4 = (bf16[1,64,64]{2,1,0:T(8,128)(2,1)S(1)}, bf16[1,64,64]{2,1,0:T(8,128)(2,1)S(1)}, u32[]{:S(2)}, u32[]{:S(2)}) collective-permute-start(bf16[1,64,64]{2,1,0:T(8,128)(2,1)S(1)} %bitcast.352), channel_id=1, source_target_pairs={{0,2},{2,4},{4,6},{6,8},{8,10},{10,12},{12,14},{1,3},{3,5},{5,7},{... | collective-permute-start | bytes 24584 | tf_op jit(solution)/shard_map/ppermute | solution.py:17
  137.6 4.5 %collective-permute-start.10 = (bf16[1,128,64]{1,2,0:T(8,128)(2,1)S(1)}, bf16[1,128,64]{1,2,0:T(8,128)(2,1)S(1)}, u32[]{:S(2)}, u32[]{:S(2)}) collective-permute-start(bf16[1,128,64]{1,2,0:T(8,128)(2,1)S(1)} %bitcast.372), channel_id=1, source_target_pairs={{0,2},{2,4},{4,6},{6,8},{8,10},{10,12},{12,14},{1,3},{3,5},{5,7},{... | collective-permute-start | bytes 49160 | tf_op jit(solution)/shard_map/ppermute | solution.py:17
  146.6 1.6 multiply_convert_fusion.2
  148.2 1.6 collective-permute-start.14
  153.1 1.5 collective-permute-done.7
  154.6 2.3 %collective-permute-start.6 = (bf16[3,1,64]{2,1,0:T(2,128)(2,1)S(1)}, bf16[3,1,64]{2,1,0:T(2,128)(2,1)S(1)}, u32[]{:S(2)}, u32[]{:S(2)}) collective-permute-start(bf16[3,1,64]{2,1,0:T(2,128)(2,1)S(1)} %get-tuple-element.17), channel_id=1, source_target_pairs={{0,1},{2,3},{4,5},{6,7},{8,9},{10,11},{12,13},{14,15},{16,17},{18,... | collective-permute-start | bytes 1160 | tf_op jit(solution)/shard_map/ppermute | solution.py:17
  159.7 1.8 fusion.31
  161.6 1.9 %fusion.33 = f32[64,128,64]{1,2,0:T(8,128)} fusion(bf16[66,130,64]{1,2,0:T(8,128)(2,1)S(1)} %select_maximum_fusion, bf16[3,3,64,64]{3,2,1,0:T(8,128)(2,1)S(1)} %get-tuple-element.15), kind=kOutput, calls=%fused_computation.66 | convolution fusion | flops 67108864 | bytes 3162112 | tf_op jit(solution)/shard_map/ijc,co->ijo/dot_general | solution.py:33
  163.5 1.9 %fusion.35 = f32[64,128,64]{1,2,0:T(8,128)} fusion(bf16[66,130,64]{1,2,0:T(8,128)(2,1)S(1)} %select_maximum_fusion, bf16[3,3,64,64]{3,2,1,0:T(8,128)(2,1)S(1)} %get-tuple-element.15), kind=kOutput, calls=%fused_computation.68 | convolution fusion | flops 67108864 | bytes 3162112 | tf_op jit(solution)/shard_map/ijc,co->ijo/dot_general | solution.py:33
  165.4 1.9 %fusion.37 = f32[64,128,64]{1,2,0:T(8,128)} fusion(bf16[66,130,64]{1,2,0:T(8,128)(2,1)S(1)} %select_maximum_fusion, bf16[3,3,64,64]{3,2,1,0:T(8,128)(2,1)S(1)} %get-tuple-element.15), kind=kOutput, calls=%fused_computation.70 | convolution fusion | flops 67108864 | bytes 3162112 | tf_op jit(solution)/shard_map/ijc,co->ijo/dot_general | solution.py:33
  167.2 1.8 fusion.39
  169.1 1.9 %fusion.29 = f32[64,128,64]{1,2,0:T(8,128)} fusion(bf16[66,130,64]{1,2,0:T(8,128)(2,1)S(1)} %select_maximum_fusion, bf16[3,3,64,64]{3,2,1,0:T(8,128)(2,1)S(1)} %get-tuple-element.15), kind=kOutput, calls=%fused_computation.62 | convolution fusion | flops 67108864 | bytes 3162112 | tf_op jit(solution)/shard_map/ijc,co->ijo/dot_general | solution.py:33
  172.2 1.8 fusion.25
  173.9 1.8 fusion.21
  176.0 8.2 %fusion.6 = bf16[1,64,128,64]{2,3,1,0:T(8,128)(2,1)} fusion(f32[64,128,64]{1,2,0:T(8,128)} %fusion.29, f32[64,128,64]{1,2,0:T(8,128)} %fusion.25, f32[64,128,64]{1,2,0:T(8,128)} %fusion.31, f32[64,128,64]{1,2,0:T(8,128)} %fusion.33, f32[64,128,64]{1,2,0:T(8,128)S(1)} %fusion.76, f32[64,128,64]{1,2,0:T(8,128)} %fusion.35, f32[64,128,64]{1,2,0:T(8,128)} %fusion.37, ...), kind=kOutput, calls=%fused_computation.12 | convolution fusion | flops 284164096 | bytes 21069824 | tf_op jit(solution)/shard_map/xyzh,hc->xyzc/dot_general | solution.py:87
  (92 shorter events, 30.8 us)
Async XLA Ops:
  0.0 176.0 %copy-start = (bf16[128,64]{0,1:T(8,128)(2,1)S(1)}, bf16[128,64]{0,1:T(8,128)(2,1)}, u32[]{:S(2)}) copy-start(bf16[128,64]{0,1:T(8,128)(2,1)} %param.15) | copy-start | bytes 49156
  1.4 1.7 copy-start.3
  1.4 9.3 %copy-start.2 = (bf16[64,64]{1,0:T(8,128)(2,1)S(1)}, bf16[64,64]{1,0:T(8,128)(2,1)}, u32[]{:S(2)}) copy-start(bf16[64,64]{1,0:T(8,128)(2,1)} %param.11) | copy-start | bytes 24580
  3.9 113.7 %collective-permute-start.1 = (bf16[1,64,64]{1,2,0:T(8,128)(2,1)S(1)}, bf16[1,64,64]{1,2,0:T(8,128)(2,1)}, u32[]{:S(2)}, u32[]{:S(2)}) collective-permute-start(bf16[1,64,64]{1,2,0:T(8,128)(2,1)S(1)} %convert_bitcast_fusion.1), channel_id=1, source_target_pairs={{2,0},{4,2},{6,4},{8,6},{10,8},{12,10},{14,12},{3,1},{5,3},{7,5},{... | collective-permute-start | bytes 24584 | tf_op jit(solution)/shard_map/ppermute | solution.py:19
  5.2 112.5 %collective-permute-start = (bf16[1,64,64]{1,2,0:T(8,128)(2,1)S(1)}, bf16[1,64,64]{1,2,0:T(8,128)(2,1)S(1)}, u32[]{:S(2)}, u32[]{:S(2)}) collective-permute-start(bf16[1,64,64]{1,2,0:T(8,128)(2,1)S(1)} %convert_bitcast_fusion.1), channel_id=1, source_target_pairs={{0,2},{2,4},{4,6},{6,8},{8,10},{10,12},{12,14},{1,3},{3,5},{5,7},{... | collective-permute-start | bytes 24584 | tf_op jit(solution)/shard_map/ppermute | solution.py:17
  15.0 112.6 %collective-permute-start.9 = (bf16[1,128,64]{1,2,0:T(8,128)(2,1)S(1)}, bf16[1,128,64]{1,2,0:T(8,128)(2,1)}, u32[]{:S(2)}, u32[]{:S(2)}) collective-permute-start(bf16[1,128,64]{1,2,0:T(8,128)(2,1)S(1)} %psum.14), channel_id=1, source_target_pairs={{2,0},{4,2},{6,4},{8,6},{10,8},{12,10},{14,12},{3,1},{5,3},{7,5},{... | collective-permute-start | bytes 49160 | tf_op jit(solution)/shard_map/ppermute | solution.py:19
  16.3 115.9 %collective-permute-start.8 = (bf16[1,128,64]{1,2,0:T(8,128)(2,1)S(1)}, bf16[1,128,64]{1,2,0:T(8,128)(2,1)}, u32[]{:S(2)}, u32[]{:S(2)}) collective-permute-start(bf16[1,128,64]{1,2,0:T(8,128)(2,1)S(1)} %psum.14), channel_id=1, source_target_pairs={{0,2},{2,4},{4,6},{6,8},{8,10},{10,12},{12,14},{1,3},{3,5},{5,7},{... | collective-permute-start | bytes 49160 | tf_op jit(solution)/shard_map/ppermute | solution.py:17
  114.5 23.2 %collective-permute-start.12 = (bf16[1,128,64]{1,2,0:T(8,128)(2,1)S(1)}, bf16[1,128,64]{1,2,0:T(8,128)(2,1)S(1)}, u32[]{:S(2)}, u32[]{:S(2)}) collective-permute-start(bf16[1,128,64]{1,2,0:T(8,128)(2,1)S(1)} %get-tuple-element.9), channel_id=1, source_target_pairs={{0,1},{2,3},{4,5},{6,7},{8,9},{10,11},{12,13},{14,15},{16,17},{18,... | collective-permute-start | bytes 49160 | tf_op jit(solution)/shard_map/ppermute | solution.py:17
  118.5 2.8 %collective-permute-start.2 = (bf16[3,1,64]{1,2,0:T(8,128)(2,1)S(1)}, bf16[3,1,64]{1,2,0:T(8,128)(2,1)S(1)}, u32[]{:S(2)}, u32[]{:S(2)}) collective-permute-start(bf16[3,1,64]{1,2,0:T(8,128)(2,1)S(1)} %get-tuple-element.21), channel_id=1, source_target_pairs={{0,1},{2,3},{4,5},{6,7},{8,9},{10,11},{12,13},{14,15},{16,17},{18,... | collective-permute-start | bytes 1160 | tf_op jit(solution)/shard_map/ppermute | solution.py:17
  119.8 3.1 %collective-permute-start.3 = (bf16[3,1,64]{1,2,0:T(8,128)(2,1)S(1)}, bf16[3,1,64]{1,2,0:T(8,128)(2,1)S(1)}, u32[]{:S(2)}, u32[]{:S(2)}) collective-permute-start(bf16[3,1,64]{1,2,0:T(8,128)(2,1)S(1)} %get-tuple-element.22), channel_id=1, source_target_pairs={{1,0},{3,2},{5,4},{7,6},{9,8},{11,10},{13,12},{15,14},{17,16},{19,... | collective-permute-start | bytes 1160 | tf_op jit(solution)/shard_map/ppermute | solution.py:19
  121.3 20.9 %collective-permute-start.13 = (bf16[1,128,64]{1,2,0:T(8,128)(2,1)S(1)}, bf16[1,128,64]{1,2,0:T(8,128)(2,1)S(1)}, u32[]{:S(2)}, u32[]{:S(2)}) collective-permute-start(bf16[1,128,64]{1,2,0:T(8,128)(2,1)S(1)} %get-tuple-element.10), channel_id=1, source_target_pairs={{1,0},{3,2},{5,4},{7,6},{9,8},{11,10},{13,12},{15,14},{17,16},{19,... | collective-permute-start | bytes 49160 | tf_op jit(solution)/shard_map/ppermute | solution.py:19
  126.2 24.0 %collective-permute-start.5 = (bf16[1,64,64]{2,1,0:T(8,128)(2,1)S(1)}, bf16[1,64,64]{2,1,0:T(8,128)(2,1)S(1)}, u32[]{:S(2)}, u32[]{:S(2)}) collective-permute-start(bf16[1,64,64]{2,1,0:T(8,128)(2,1)S(1)} %bitcast.351), channel_id=1, source_target_pairs={{2,0},{4,2},{6,4},{8,6},{10,8},{12,10},{14,12},{3,1},{5,3},{7,5},{... | collective-permute-start | bytes 24584 | tf_op jit(solution)/shard_map/ppermute | solution.py:19
  127.6 23.9 %collective-permute-start.4 = (bf16[1,64,64]{2,1,0:T(8,128)(2,1)S(1)}, bf16[1,64,64]{2,1,0:T(8,128)(2,1)S(1)}, u32[]{:S(2)}, u32[]{:S(2)}) collective-permute-start(bf16[1,64,64]{2,1,0:T(8,128)(2,1)S(1)} %bitcast.352), channel_id=1, source_target_pairs={{0,2},{2,4},{4,6},{6,8},{8,10},{10,12},{12,14},{1,3},{3,5},{5,7},{... | collective-permute-start | bytes 24584 | tf_op jit(solution)/shard_map/ppermute | solution.py:17
  136.3 21.7 %collective-permute-start.11 = (bf16[1,128,64]{1,2,0:T(8,128)(2,1)S(1)}, bf16[1,128,64]{1,2,0:T(8,128)(2,1)S(1)}, u32[]{:S(2)}, u32[]{:S(2)}) collective-permute-start(bf16[1,128,64]{1,2,0:T(8,128)(2,1)S(1)} %bitcast.371), channel_id=1, source_target_pairs={{2,0},{4,2},{6,4},{8,6},{10,8},{12,10},{14,12},{3,1},{5,3},{7,5},{... | collective-permute-start | bytes 49160 | tf_op jit(solution)/shard_map/ppermute | solution.py:19
  137.6 20.4 %collective-permute-start.10 = (bf16[1,128,64]{1,2,0:T(8,128)(2,1)S(1)}, bf16[1,128,64]{1,2,0:T(8,128)(2,1)S(1)}, u32[]{:S(2)}, u32[]{:S(2)}) collective-permute-start(bf16[1,128,64]{1,2,0:T(8,128)(2,1)S(1)} %bitcast.372), channel_id=1, source_target_pairs={{0,2},{2,4},{4,6},{6,8},{8,10},{10,12},{12,14},{1,3},{3,5},{5,7},{... | collective-permute-start | bytes 49160 | tf_op jit(solution)/shard_map/ppermute | solution.py:17
  148.2 10.4 %collective-permute-start.14 = (bf16[1,128,64]{1,2,0:T(8,128)(2,1)S(1)}, bf16[1,128,64]{1,2,0:T(8,128)(2,1)S(1)}, u32[]{:S(2)}, u32[]{:S(2)}) collective-permute-start(bf16[1,128,64]{1,2,0:T(8,128)(2,1)S(1)} %get-tuple-element.7), channel_id=1, source_target_pairs={{0,1},{2,3},{4,5},{6,7},{8,9},{10,11},{12,13},{14,15},{16,17},{18,... | collective-permute-start | bytes 49160 | tf_op jit(solution)/shard_map/ppermute | solution.py:17
  150.2 8.3 %collective-permute-start.15 = (bf16[1,128,64]{1,2,0:T(8,128)(2,1)S(1)}, bf16[1,128,64]{1,2,0:T(8,128)(2,1)S(1)}, u32[]{:S(2)}, u32[]{:S(2)}) collective-permute-start(bf16[1,128,64]{1,2,0:T(8,128)(2,1)S(1)} %get-tuple-element.8), channel_id=1, source_target_pairs={{1,0},{3,2},{5,4},{7,6},{9,8},{11,10},{13,12},{15,14},{17,16},{19,... | collective-permute-start | bytes 49160 | tf_op jit(solution)/shard_map/ppermute | solution.py:19
  151.6 3.0 %collective-permute-start.7 = (bf16[3,1,64]{2,1,0:T(2,128)(2,1)S(1)}, bf16[3,1,64]{2,1,0:T(2,128)(2,1)S(1)}, u32[]{:S(2)}, u32[]{:S(2)}) collective-permute-start(bf16[3,1,64]{2,1,0:T(2,128)(2,1)S(1)} %get-tuple-element.18), channel_id=1, source_target_pairs={{1,0},{3,2},{5,4},{7,6},{9,8},{11,10},{13,12},{15,14},{17,16},{19,... | collective-permute-start | bytes 1160 | tf_op jit(solution)/shard_map/ppermute | solution.py:19
  154.6 2.9 %collective-permute-start.6 = (bf16[3,1,64]{2,1,0:T(2,128)(2,1)S(1)}, bf16[3,1,64]{2,1,0:T(2,128)(2,1)S(1)}, u32[]{:S(2)}, u32[]{:S(2)}) collective-permute-start(bf16[3,1,64]{2,1,0:T(2,128)(2,1)S(1)} %get-tuple-element.17), channel_id=1, source_target_pairs={{0,1},{2,3},{4,5},{6,7},{8,9},{10,11},{12,13},{14,15},{16,17},{18,... | collective-permute-start | bytes 1160 | tf_op jit(solution)/shard_map/ppermute | solution.py:17
  173.9 2.0 %copy-start.1 = (bf16[1,64,128,64]{2,3,1,0:T(8,128)(2,1)S(1)}, bf16[1,64,128,64]{2,3,1,0:T(8,128)(2,1)}, u32[]{:S(2)}) copy-start(bf16[1,64,128,64]{2,3,1,0:T(8,128)(2,1)} %param.8) | copy-start | bytes 3145732
where the time goes:
time: 185 us; the launch traced here: 184 us
  blocking collectives  95.5 us (52%)
  matrix products  38.9 us (21%)
  starting transfers between devices  37.3 us (20%)
  other arithmetic  8.05 us (4%)
  waiting for transfers between devices  2.25 us (1%)
    psum x1, blocking collectives, shards(): yz_plane = lax.psum(yz_part, 'gx').astype(jnp.bfloat16)  92.1 us
    dot_general x54, matrix products, conv_valid(): jnp.einsum('ijc,co->ijo', window, kernel[row_off, col_off], preferred_ele...  29.1 us
    ppermute x8, starting transfers between devices, with_halo(): lax.ppermute(tail, axis, [(i, (i + 1) % count) for i in range(ends)])  27 us
    ppermute x8, starting transfers between devices, with_halo(): lax.ppermute(head, axis, [((i + 1) % count, i) for i in range(ends)])  10.3 us
    dot_general x1, matrix products, shards(): jnp.einsum('xyzh,hc->xyzc', hidden, shrink_weight, preferred_element_type...  8.17 us
    concatenate x6, other arithmetic, with_halo(): jnp.concatenate([lax.ppermute(tail, axis, [(i, (i + 1) % count) for i in...  4.91 us
  transfers between devices with their start and end apart: 16, of which 3 were waited for; matrix products, arithmetic and copies ran while one was open for 10% of the time, Pallas kernels for 0%

commit v1 on v0

--- a/solution.py
+++ b/solution.py
@@ -1,9 +1,15 @@
+import functools
+
 import jax
 import jax.numpy as jnp
 from jax import lax
+from jax.experimental import pallas as pl
+from jax.experimental.pallas import tpu as pltpu
 from jax.sharding import PartitionSpec as P
 
 product_scale = 8.0
+f32 = jnp.float32
+bf16 = jnp.bfloat16
 
 
 def with_halo(cells, sides, width):
@@ -55,7 +61,7 @@
     return jnp.pad(padded, ((0, 0), (1, 1), (0, 0)))
 
 
-def shards(
+def general(
     voxels,
     occupancy,
     row_weights,
@@ -88,6 +94,248 @@
     return (features.astype(jnp.float32) + branch).astype(jnp.bfloat16)
 
 
+def silu(v):
+    half = 0.5 * v
+    return half * jnp.tanh(half) + half
+
+
+def taps(rows):
+    n, c, w = rows.shape
+    wide = rows.astype(f32).reshape(n * c, w)
+    lane = lax.broadcasted_iota(jnp.int32, (n * c, w), 1)
+    left = jnp.where(lane == 0, 0.0, pltpu.roll(wide, 1, 1)).astype(bf16).reshape(n, c, w)
+    right = jnp.where(lane == w - 1, 0.0, pltpu.roll(wide, w - 1, 1)).astype(bf16).reshape(n, c, w)
+    parts = [jnp.concatenate([left[i], rows[i], right[i]], axis=0) for i in range(n)]
+    return jnp.concatenate(parts, axis=1)
+
+
+def conv_rows(rows, weight):
+    n, c, w = rows.shape
+    full = jnp.dot(weight, taps(rows), preferred_element_type=f32)
+    o = weight.shape[0] // 3
+    out = []
+    for i in range(n - 2):
+        out.append(
+            full[0:o, i * w : (i + 1) * w]
+            + full[o : 2 * o, (i + 1) * w : (i + 2) * w]
+            + full[2 * o : 3 * o, (i + 2) * w : (i + 3) * w]
+        )
+    return out
+
+
+def place():
+    return lax.axis_index("gx") % 4, lax.axis_index("gy")
+
+
+def front_kernel(row_ref, vox_ref, occ_ref, *out_refs, chunk):
+    rows, c, z = vox_ref.shape
+    low, core = place()
+    base = chunk_base(chunk, core, rows)
+    quarter = rows // 8
+    weight = row_ref[...].astype(f32)
+    for d in (1, 2, 3, 0):
+        first = base + jnp.bitwise_xor(low, d) * quarter
+        occ = occ_ref[pl.ds(first, quarter)].astype(f32)
+        for i in range(quarter):
+            value = vox_ref[first + i].astype(f32) * occ[i : i + 1] * weight
+            out_refs[d][i] = value.astype(out_refs[d].dtype)
+
+
+def chunk_base(chunk, core, rows):
+    half = rows // 2
+    return (1 - core) * half if chunk == 0 else core * half
+
+
+def sums_kernel(vox_ref, occ_ref, column_ref, depth_ref, after_ref, out_ref):
+    del after_ref
+    rows, c, z = vox_ref.shape
+    depth = depth_ref[...].astype(f32)
+    column = column_ref[...].astype(f32)
+    lane = lax.broadcasted_iota(jnp.int32, (c, rows), 1)
+    xz = jnp.zeros((c, z), f32)
+    xy = jnp.zeros((c, rows), f32)
+    for y in range(rows):
+        feats = vox_ref[y].astype(f32) * occ_ref[y : y + 1].astype(f32)
+        xz = xz + feats * column[:, y : y + 1]
+        xy = jnp.where(lane == y, jnp.sum(feats * depth, axis=1, keepdims=True), xy)
+    out_ref[:, :z] = xz
+    out_ref[:, z:] = xy.astype(bf16).astype(f32)
+
+
+def planes_kernel(own_ref, other_ref, after_ref, out_ref):
+    del after_ref
+    z = out_ref.shape[2]
+    _, core = place()
+    own, other = own_ref[...], other_ref[...]
+    own_xy, other_xy = own[:, z:], other[:, z:]
+    first = jnp.where(core == 0, own_xy, other_xy)
+    second = jnp.where(core == 0, other_xy, own_xy)
+    out_ref[0] = jnp.concatenate([first, second], axis=1).astype(bf16)
+    out_ref[1] = (own[:, :z] + other[:, :z]).astype(bf16)
+
+
+def weights_kernel(kernel_ref, after_ref, out_ref):
+    del after_ref
+    for p in range(kernel_ref.shape[0]):
+        for l in range(kernel_ref.shape[1]):
+            for a in range(3):
+                rows = jnp.concatenate([kernel_ref[p, l, a, b] for b in range(3)], axis=0)
+                o = rows.shape[1]
+                out_ref[p, l, a * o : (a + 1) * o] = rows.astype(f32).T.astype(bf16)
+
+
+def small_kernel(*refs, last):
+    near_refs, weight_ref, after_ref, out_ref = refs[:5], refs[5], refs[6], refs[7]
+    del after_ref
+    at = lax.axis_index("gx")
+    _, core = place()
+    valid = [jnp.where(at > 0, 1.0, 0.0), 1.0, jnp.where(at < last, 1.0, 0.0)]
+    for p in range(2):
+        rows = jnp.stack([ref[p] for ref in near_refs])
+        inner = conv_rows(rows, weight_ref[p, 0])
+        inner = jnp.stack([(silu(v) * valid[i]).astype(bf16) for i, v in enumerate(inner)])
+        value = conv_rows(inner, weight_ref[p, 1])[0]
+        if p == 0:
+            value = jnp.where(core == 0, value, pltpu.roll(value, value.shape[1] // 2, 1))
+        out_ref[p] = value.astype(bf16)
+
+
+def main_kernel(*refs, group):
+    pieces, (halo_ref, vox_ref, occ_ref, small_ref, weight_ref, expand_ref, shrink_ref) = refs[:8], refs[8:15]
+    out_ref, plane_ref, inner_ref = refs[15:]
+    rows, c, z = vox_ref.shape
+    low, core = place()
+    quarter = rows // 8
+    top = jnp.where(core == 0, 0.0, 1.0)
+    bottom = 1.0 - top
+    halo = halo_ref[...].astype(f32)
+    plane_ref[0:2] = (halo * top).astype(bf16)
+    plane_ref[rows + 2 : rows + 4] = (halo * bottom).astype(bf16)
+    for chunk in range(2):
+        for d in range(4):
+            first = 2 + chunk_base(chunk, core, rows) + jnp.bitwise_xor(low, d) * quarter
+            plane_ref[pl.ds(first, quarter)] = pieces[4 * chunk + d][...]
+    in_group = (rows + 2) // 3 if (rows + 2) % 3 == 0 else rows + 2
+    for g in range((rows + 2) // in_group):
+        base = g * in_group
+        outs = conv_rows(plane_ref[base : base + in_group + 2], weight_ref[0])
+        for i, v in enumerate(outs):
+            v = silu(v)
+            if base + i == 0:
+                v = v * top
+            if base + i == rows + 1:
+                v = v * bottom
+            inner_ref[base + i] = v.astype(bf16)
+    xz = small_ref[1].astype(f32)
+    xy = small_ref[0].astype(f32)
+    for g in range(rows // group):
+        base = g * group
+        outs = conv_rows(inner_ref[base : base + group + 2], weight_ref[1])
+        mixed = []
+        for i, v in enumerate(outs):
+            y = base + i
+            product = xy[:, y : y + 1] * xz * v.astype(bf16).astype(f32)
+            mixed.append((product_scale * product).astype(bf16))
+        mixed = jnp.concatenate(mixed, axis=1)
+        hidden = silu(jnp.dot(expand_ref[...], mixed, preferred_element_type=f32)).astype(bf16)
+        branch = jnp.dot(shrink_ref[...], hidden, preferred_element_type=f32)
+        for i in range(group):
+            y = base + i
+            feats = vox_ref[y].astype(f32) * occ_ref[y : y + 1].astype(f32)
+            out_ref[y] = (feats + branch[:, i * z : (i + 1) * z]).astype(bf16)
+
+
+def swap(value, axis, bit):
+    return lax.ppermute(value, axis, [(i, i ^ bit) for i in range(lax.axis_size(axis))])
+
+
+def shifted(value, axis, by):
+    size = lax.axis_size(axis)
+    pairs = [(i, i - by) for i in range(size) if 0 <= i - by < size]
+    return lax.ppermute(value, axis, pairs)
+
+
+def vmem():
+    return pl.BlockSpec(memory_space=pltpu.VMEM)
+
+
+def anywhere():
+    return pl.BlockSpec(memory_space=pl.ANY)
+
+
+def call(kernel, name, out_shape, specs, scratch=()):
+    return pl.pallas_call(
+        kernel,
+        out_shape=out_shape,
+        in_specs=specs,
+        out_specs=jax.tree.map(lambda _: vmem(), out_shape),
+        scratch_shapes=list(scratch),
+        compiler_params=pltpu.CompilerParams(vmem_limit_bytes=40 * 1024 * 1024),
+        name=name,
+    )
+
+
+def shards(
+    voxels, occupancy, row_weights, column_weights, depth_weights, plane_kernels, expand_weight, shrink_weight
+):
+    vox = voxels.transpose(0, 1, 3, 2)[0]
+    occ = occupancy[0]
+    rows, c, z = vox.shape
+    low, core = place()
+    quarter = rows // 8
+    gx_size = lax.axis_size("gx")
+
+    row_column = jnp.broadcast_to(row_weights[0][:, None], (c, z))
+    piece = lambda kind: jax.ShapeDtypeStruct((quarter, c, z), kind)
+    totals, arrived = [], []
+    for chunk in range(2):
+        own, *send = call(
+            functools.partial(front_kernel, chunk=chunk), f"front{chunk}", [piece(f32)] + [piece(bf16)] * 3, [vmem()] * 3
+        )(row_column, vox, occ)
+        got = [swap(value, "gx", d) for d, value in zip((1, 2, 3), send)]
+        arrived.append(got)
+        totals.append((own + got[0].astype(f32) + got[1].astype(f32) + got[2].astype(f32)).astype(bf16))
+    bit = 4
+    while bit < gx_size:
+        totals = [(t.astype(f32) + swap(t, "gx", bit).astype(f32)).astype(bf16) for t in totals]
+        bit *= 2
+    pieces = [[t] + [swap(t, "gx", d) for d in (1, 2, 3)] for t in totals]
+    edge = jnp.bitwise_xor(low, jnp.where(core == 0, 3, 0))
+    beside = pieces[0][0]
+    for d in (1, 2, 3):
+        beside = jnp.where(edge == d, pieces[0][d], beside)
+    halo = swap(jnp.where(core == 0, beside[quarter - 2 :], beside[:2]), "gy", 1)
+
+    message = call(
+        sums_kernel, "sums", jax.ShapeDtypeStruct((c, z + rows), f32), [vmem()] * 4 + [anywhere()]
+    )(vox, occ, column_weights.T, depth_weights.T, arrived[0][0])
+    weights = call(
+        weights_kernel,
+        "weights",
+        jax.ShapeDtypeStruct(plane_kernels.shape[:2] + (3 * c, 3 * c), bf16),
+        [vmem(), anywhere()],
+    )(plane_kernels, arrived[0][1])
+    planes = call(
+        planes_kernel, "planes", jax.ShapeDtypeStruct((2, c, z), bf16), [vmem()] * 2 + [anywhere()]
+    )(message, swap(message, "gy", 1), totals[0])
+    near = [shifted(planes, "gx", by) if by else planes for by in (-2, -1, 0, 1, 2)]
+    small = call(
+        functools.partial(small_kernel, last=gx_size - 1),
+        "small",
+        jax.ShapeDtypeStruct(planes.shape, bf16),
+        [vmem()] * 6 + [anywhere()],
+    )(*near, weights[:2], totals[1])
+
+    out = call(
+        functools.partial(main_kernel, group=16),
+        "block",
+        jax.ShapeDtypeStruct((rows, c, z), bf16),
+        [vmem()] * 15,
+        [pltpu.VMEM((rows + 4, c, z), bf16), pltpu.VMEM((rows + 2, c, z), bf16)],
+    )(*pieces[0], *pieces[1], halo, vox, occ, small, weights[2], expand_weight.T, shrink_weight.T)
+    return out[None].transpose(0, 1, 3, 2)
+
+
 def solution(mesh):
     in_specs = (
         P(("groups", "gx"), "gy", None, None),
@@ -100,4 +348,13 @@
         P(),
     )
     out_specs = P(("groups", "gx"), "gy", None, None)
-    return jax.shard_map(shards, mesh=mesh, in_specs=in_specs, out_specs=out_specs, check_vma=False)
+
+    def whole(voxels, *rest):
+        gx, gy = mesh.shape["gx"], mesh.shape["gy"]
+        x, y, z = voxels.shape[0] // mesh.shape["groups"], voxels.shape[1], voxels.shape[2]
+        fits = gy == 2 and gx >= 4 and gx & (gx - 1) == 0 and x == gx and y == z and z == 128 and y % 32 == 0
+        part = shards if fits else general
+        mapped = jax.shard_map(part, mesh=mesh, in_specs=in_specs, out_specs=out_specs, check_vma=False)
+        return mapped(voxels, *rest)
+
+    return whole

time: 185 us -> 56.9 us (0.31)
  blocking collectives: 95.5 us -> 0 us
  matrix products: 38.9 us -> 0 us
  Pallas kernels: 0 us -> 9.54 us
  waiting for transfers between devices: 2.25 us -> 10.6 us
  other arithmetic: 8.05 us -> 0.25 us
  starting transfers between devices: 37.3 us -> 32.1 us
  local copies, waits for them, and re-layouts: 1.66 us -> 3.68 us
    psum x2 -> x0, blocking collectives: 95.5 us -> none  [the longest x1 92.1 us: shards(): yz_plane = lax.psum(yz_part, 'gx').astype(jnp.bfloat16)]
    dot_general x57 -> x0, matrix products: 38.9 us -> none  [the longest x54 29.1 us: conv_valid(): jnp.einsum('ijc,co->ijo', window, kernel[row_off, col_off], preferred_ele...]
    pallas_call x0 -> x7, Pallas kernels: none -> 9.54 us  [the longest x1 5.08 us: shards(): call(functools.partial(main_kernel, group=16), 'block', jax.ShapeDtypeStr...]
    ppermute x16 -> x20, waiting for transfers between devices: 2.25 us -> 10.6 us  [the longest x16 10.6 us: swap(): lax.ppermute(value, axis, [(i, i ^ bit) for i in range(lax.axis_size(axis...]
    ppermute x16 -> x20, starting transfers between devices: 37.3 us -> 32.1 us  [the longest x16 22 us: swap(): lax.ppermute(value, axis, [(i, i ^ bit) for i in range(lax.axis_size(axis...]
    concatenate x6 -> x0, other arithmetic: 4.91 us -> none  [with_halo(): jnp.concatenate([lax.ppermute(tail, axis, [(i, (i + 1) % count) for i in...]
    unnamed x10 -> x22, local copies, waits for them, and re-layouts: 0.26 us -> 3.57 us
  transfers between devices with their start and end apart: 16 -> 20, of which waited for: 3 -> 5; matrix products, arithmetic and copies ran while one was open for 10% -> 1% of each run, Pallas kernels for 0% -> 8%
where the time goes in v1:
time: 56.9 us; the launch traced here: 56.5 us
  starting transfers between devices  32.1 us (56%)
  waiting for transfers between devices  10.6 us (19%)
  Pallas kernels  9.54 us (17%)
  local copies, waits for them, and re-layouts  3.68 us (6%)
    ppermute x16, starting transfers between devices, swap(): lax.ppermute(value, axis, [(i, i ^ bit) for i in range(lax.axis_size(axis...  22 us
    ppermute x16, waiting for transfers between devices, swap(): lax.ppermute(value, axis, [(i, i ^ bit) for i in range(lax.axis_size(axis...  10.6 us
    ppermute x4, starting transfers between devices, shifted(): return lax.ppermute(value, axis, pairs)  10.2 us
    pallas_call x1, Pallas kernels, shards(): call(functools.partial(main_kernel, group=16), 'block', jax.ShapeDtypeStr...  5.08 us
    unnamed x22, local copies, waits for them, and re-layouts  3.57 us
    pallas_call x1, Pallas kernels, shards(): call(sums_kernel, 'sums', jax.ShapeDtypeStruct((c, z + rows), f32), [vmem...  2.91 us
  transfers between devices with their start and end apart: 20, of which 5 were waited for; matrix products, arithmetic and copies ran while one was open for 1% of the time, Pallas kernels for 8%

profile of v1, /device:TPU:0, one launch (start us, length us, event | category | flops | bytes accessed | tf_op | source)
XLA Modules:
  0.0 56.5 jit_solution(15923552161962236347)
XLA Ops:
  0.7 1.2 %copy-done = bf16[1,64,128,64]{2,3,1,0:T(8,128)(2,1)S(1)} copy-done((bf16[1,64,128,64]{2,3,1,0:T(8,128)(2,1)S(1)}, bf16[1,64,128,64]{2,3,1,0:T(8,128)(2,1)}, u32[]{:S(2)}) %copy-start) | copy-done | bytes 1048600
  2.0 0.8 %copy-done.3 = s32[1,64,128]{2,1,0:T(8,128)S(1)} copy-done((s32[1,64,128]{2,1,0:T(8,128)S(1)}, s32[1,64,128]{2,1,0:T(8,128)}, u32[]{:S(2)}) %copy-start.3) | copy-done | bytes 32792
  2.9 3.0 %collective-permute-start = (bf16[8,64,128]{2,1,0:T(8,128)(2,1)S(1)}, bf16[8,64,128]{2,1,0:T(8,128)(2,1)S(1)}, u32[]{:S(2)}, u32[]{:S(2)}) collective-permute-start(bf16[8,64,128]{2,1,0:T(8,128)(2,1)S(1)} %get-tuple-element.14), channel_id=1, source_target_pairs={{0,2},{2,0},{4,6},{6,4},{8,10},{10,8},{12,14},{14,12},{1,3},{3,1},... | collective-permute-start | bytes 393224 | tf_op jit(solution)/shard_map/ppermute | solution.py:249
  5.9 1.6 %collective-permute-start.1 = (bf16[8,64,128]{2,1,0:T(8,128)(2,1)S(1)}, bf16[8,64,128]{2,1,0:T(8,128)(2,1)S(1)}, u32[]{:S(2)}, u32[]{:S(2)}) collective-permute-start(bf16[8,64,128]{2,1,0:T(8,128)(2,1)S(1)} %get-tuple-element.15), channel_id=1, source_target_pairs={{0,4},{2,6},{4,0},{6,2},{8,12},{10,14},{12,8},{14,10},{1,5},{3,7},... | collective-permute-start | bytes 393224 | tf_op jit(solution)/shard_map/ppermute | solution.py:249
  7.6 2.0 %collective-permute-start.7 = (bf16[8,64,128]{2,1,0:T(8,128)(2,1)S(1)}, bf16[8,64,128]{2,1,0:T(8,128)(2,1)S(1)}, u32[]{:S(2)}, u32[]{:S(2)}) collective-permute-start(bf16[8,64,128]{2,1,0:T(8,128)(2,1)S(1)} %get-tuple-element.18), channel_id=1, source_target_pairs={{0,2},{2,0},{4,6},{6,4},{8,10},{10,8},{12,14},{14,12},{1,3},{3,1},... | collective-permute-start | bytes 393224 | tf_op jit(solution)/shard_map/ppermute | solution.py:249
  9.6 1.6 %collective-permute-start.8 = (bf16[8,64,128]{2,1,0:T(8,128)(2,1)S(1)}, bf16[8,64,128]{2,1,0:T(8,128)(2,1)S(1)}, u32[]{:S(2)}, u32[]{:S(2)}) collective-permute-start(bf16[8,64,128]{2,1,0:T(8,128)(2,1)S(1)} %get-tuple-element.19), channel_id=1, source_target_pairs={{0,4},{2,6},{4,0},{6,2},{8,12},{10,14},{12,8},{14,10},{1,5},{3,7},... | collective-permute-start | bytes 393224 | tf_op jit(solution)/shard_map/ppermute | solution.py:249
  11.3 0.7 %copy-done.7 = bf16[64,128]{1,0:T(8,128)(2,1)S(1)} copy-done((bf16[64,128]{1,0:T(8,128)(2,1)S(1)}, bf16[64,128]{1,0:T(8,128)(2,1)}, u32[]{:S(2)}) %copy-start.7) | copy-done | bytes 16408
  12.5 2.3 %collective-permute-done.2 = bf16[8,64,128]{2,1,0:T(8,128)(2,1)S(1)} collective-permute-done((bf16[8,64,128]{2,1,0:T(8,128)(2,1)S(1)}, bf16[8,64,128]{2,1,0:T(8,128)(2,1)S(1)}, u32[]{:S(2)}, u32[]{:S(2)}) %collective-permute-start.2) | collective-permute-done | bytes 131104 | tf_op jit(solution)/shard_map/ppermute | solution.py:249
  14.9 2.6 %collective-permute-start.3 = (bf16[8,64,128]{2,1,0:T(8,128)(2,1)S(1)}, bf16[8,64,128]{2,1,0:T(8,128)(2,1)S(1)}, u32[]{:S(2)}, u32[]{:S(2)}) collective-permute-start(bf16[8,64,128]{2,1,0:T(8,128)(2,1)S(1)} %add_convert_fusion.3), channel_id=1, source_target_pairs={{0,8},{2,10},{4,12},{6,14},{8,0},{10,2},{12,4},{14,6},{1,9},{3,11}... | collective-permute-start | bytes 393224 | tf_op jit(solution)/shard_map/ppermute | solution.py:249
  17.5 2.9 %sums.1.own_ref = f32[64,192]{1,0:T(8,128)S(1)} custom-call(bf16[64,64,128]{2,1,0:T(8,128)(2,1)S(1)} %bitcast.16, s32[64,128]{1,0:T(8,128)S(1)} %bitcast.20, bf16[64,64]{1,0:T(8,128)(2,1)S(1)} %bitcast.23, bf16[64,128]{1,0:T(8,128)(2,1)S(1)} %bitcast.24, bf16[8,64,128]{2,1,0:T(8,128)(2,1)S(1)} %collective-permute-done.after_ref), custom_call_target="tpu_custom_call" | custom-call | tf_op jit(solution)/shard_map/sums/pallas_call | solution.py:309
  20.6 2.5 %collective-permute-start.10 = (bf16[8,64,128]{2,1,0:T(8,128)(2,1)S(1)}, bf16[8,64,128]{2,1,0:T(8,128)(2,1)S(1)}, u32[]{:S(2)}, u32[]{:S(2)}) collective-permute-start(bf16[8,64,128]{2,1,0:T(8,128)(2,1)S(1)} %add_convert_fusion.1), channel_id=1, source_target_pairs={{0,8},{2,10},{4,12},{6,14},{8,0},{10,2},{12,4},{14,6},{1,9},{3,11}... | collective-permute-start | bytes 393224 | tf_op jit(solution)/shard_map/ppermute | solution.py:249
  23.6 3.7 %collective-permute-start.16 = (bf16[2,64,128]{2,1,0:T(8,128)(2,1)S(1)}, bf16[2,64,128]{2,1,0:T(8,128)(2,1)S(1)}, u32[]{:S(2)}, u32[]{:S(2)}) collective-permute-start(bf16[2,64,128]{2,1,0:T(8,128)(2,1)S(1)} %planes.1.refs_2_), channel_id=1, source_target_pairs={{0,4},{2,6},{4,8},{6,10},{8,12},{10,14},{1,5},{3,7},{5,9},{7,11},{... | collective-permute-start | bytes 98312 | tf_op jit(solution)/shard_map/ppermute | solution.py:255
  27.3 3.9 %collective-permute-start.17 = (bf16[2,64,128]{2,1,0:T(8,128)(2,1)S(1)}, bf16[2,64,128]{2,1,0:T(8,128)(2,1)S(1)}, u32[]{:S(2)}, u32[]{:S(2)}) collective-permute-start(bf16[2,64,128]{2,1,0:T(8,128)(2,1)S(1)} %planes.1.refs_2_), channel_id=1, source_target_pairs={{0,2},{2,4},{4,6},{6,8},{8,10},{10,12},{12,14},{1,3},{3,5},{5,7},{... | collective-permute-start | bytes 98312 | tf_op jit(solution)/shard_map/ppermute | solution.py:255
  31.3 3.3 %collective-permute-start.5 = (bf16[8,64,128]{2,1,0:T(8,128)(2,1)S(1)}, bf16[8,64,128]{2,1,0:T(8,128)(2,1)S(1)}, u32[]{:S(2)}, u32[]{:S(2)}) collective-permute-start(bf16[8,64,128]{2,1,0:T(8,128)(2,1)S(1)} %add_convert_fusion.2.after_ref.refs_0_), channel_id=1, source_target_pairs={{0,4},{2,6},{4,0},{6,2},{8,12},{10,14},{12,8},{14,10},{1,5},{3,7},... | collective-permute-start | bytes 393224 | tf_op jit(solution)/shard_map/ppermute | solution.py:249
  34.8 2.6 %collective-permute-done.4.refs_1_ = bf16[8,64,128]{2,1,0:T(8,128)(2,1)S(1)} collective-permute-done((bf16[8,64,128]{2,1,0:T(8,128)(2,1)S(1)}, bf16[8,64,128]{2,1,0:T(8,128)(2,1)S(1)}, u32[]{:S(2)}, u32[]{:S(2)}) %collective-permute-start.4) | collective-permute-done | bytes 131104 | tf_op jit(solution)/shard_map/ppermute | solution.py:249
  37.4 1.3 %collective-permute-start.18 = (bf16[2,64,128]{2,1,0:T(8,128)(2,1)S(1)}, bf16[2,64,128]{2,1,0:T(8,128)(2,1)S(1)}, u32[]{:S(2)}, u32[]{:S(2)}) collective-permute-start(bf16[2,64,128]{2,1,0:T(8,128)(2,1)S(1)} %planes.1.refs_2_), channel_id=1, source_target_pairs={{2,0},{4,2},{6,4},{8,6},{10,8},{12,10},{14,12},{3,1},{5,3},{7,5},{... | collective-permute-start | bytes 98312 | tf_op jit(solution)/shard_map/ppermute | solution.py:255
  38.7 1.3 %collective-permute-start.19 = (bf16[2,64,128]{2,1,0:T(8,128)(2,1)S(1)}, bf16[2,64,128]{2,1,0:T(8,128)(2,1)S(1)}, u32[]{:S(2)}, u32[]{:S(2)}) collective-permute-start(bf16[2,64,128]{2,1,0:T(8,128)(2,1)S(1)} %planes.1.refs_2_), channel_id=1, source_target_pairs={{4,0},{6,2},{8,4},{10,6},{12,8},{14,10},{5,1},{7,3},{9,5},{11,7},{... | collective-permute-start | bytes 98312 | tf_op jit(solution)/shard_map/ppermute | solution.py:255
  40.0 0.8 %collective-permute-done.6.refs_3_ = bf16[8,64,128]{2,1,0:T(8,128)(2,1)S(1)} collective-permute-done((bf16[8,64,128]{2,1,0:T(8,128)(2,1)S(1)}, bf16[8,64,128]{2,1,0:T(8,128)(2,1)S(1)}, u32[]{:S(2)}, u32[]{:S(2)}) %collective-permute-start.6) | collective-permute-done | bytes 131104 | tf_op jit(solution)/shard_map/ppermute | solution.py:249
  40.8 1.9 %collective-permute-start.11 = (bf16[8,64,128]{2,1,0:T(8,128)(2,1)S(1)}, bf16[8,64,128]{2,1,0:T(8,128)(2,1)S(1)}, u32[]{:S(2)}, u32[]{:S(2)}) collective-permute-start(bf16[8,64,128]{2,1,0:T(8,128)(2,1)S(1)} %add_convert_fusion.refs_6_.refs_4_), channel_id=1, source_target_pairs={{0,2},{2,0},{4,6},{6,4},{8,10},{10,8},{12,14},{14,12},{1,3},{3,1},... | collective-permute-start | bytes 393224 | tf_op jit(solution)/shard_map/ppermute | solution.py:249
  42.8 2.7 %collective-permute-start.12 = (bf16[8,64,128]{2,1,0:T(8,128)(2,1)S(1)}, bf16[8,64,128]{2,1,0:T(8,128)(2,1)S(1)}, u32[]{:S(2)}, u32[]{:S(2)}) collective-permute-start(bf16[8,64,128]{2,1,0:T(8,128)(2,1)S(1)} %add_convert_fusion.refs_6_.refs_4_), channel_id=1, source_target_pairs={{0,4},{2,6},{4,0},{6,2},{8,12},{10,14},{12,8},{14,10},{1,5},{3,7},... | collective-permute-start | bytes 393224 | tf_op jit(solution)/shard_map/ppermute | solution.py:249
  45.7 0.9 %small.1.refs_11_ = bf16[2,64,128]{2,1,0:T(8,128)(2,1)S(1)} custom-call(bf16[2,64,128]{2,1,0:T(8,128)(2,1)S(1)} %collective-permute-done.16.refs_0_, bf16[2,64,128]{2,1,0:T(8,128)(2,1)S(1)} %collective-permute-done.17.refs_1_, bf16[2,64,128]{2,1,0:T(8,128)(2,1)S(1)} %planes.1.refs_2_, bf16[2,64,128]{2,1,0:T(8,128)(2,1)S(1)} %collective-permute-done.18.refs_3_, ...), custom_call_target="tpu_custom_call" | custom-call | tf_op jit(solution)/shard_map/small/pallas_call | solution.py:322
  46.6 1.8 %collective-permute-done.12.refs_6_ = bf16[8,64,128]{2,1,0:T(8,128)(2,1)S(1)} collective-permute-done((bf16[8,64,128]{2,1,0:T(8,128)(2,1)S(1)}, bf16[8,64,128]{2,1,0:T(8,128)(2,1)S(1)}, u32[]{:S(2)}, u32[]{:S(2)}) %collective-permute-start.12) | collective-permute-done | bytes 131104 | tf_op jit(solution)/shard_map/ppermute | solution.py:249
  48.5 2.9 %collective-permute-done.13.refs_7_ = bf16[8,64,128]{2,1,0:T(8,128)(2,1)S(1)} collective-permute-done((bf16[8,64,128]{2,1,0:T(8,128)(2,1)S(1)}, bf16[8,64,128]{2,1,0:T(8,128)(2,1)S(1)}, u32[]{:S(2)}, u32[]{:S(2)}) %collective-permute-start.13) | collective-permute-done | bytes 131104 | tf_op jit(solution)/shard_map/ppermute | solution.py:249
  51.4 5.1 %block.1 = bf16[64,64,128]{2,1,0:T(8,128)(2,1)} custom-call(bf16[8,64,128]{2,1,0:T(8,128)(2,1)S(1)} %add_convert_fusion.2.after_ref.refs_0_, bf16[8,64,128]{2,1,0:T(8,128)(2,1)S(1)} %collective-permute-done.4.refs_1_, bf16[8,64,128]{2,1,0:T(8,128)(2,1)S(1)} %collective-permute-done.5.refs_2_, bf16[8,64,128]{2,1,0:T(8,128)(2,1)S(1)} %collective-permute-done.6.refs_3_, ...), custom_call_target="tpu_custom_call" | custom-call | tf_op jit(solution)/shard_map/block/pallas_call | solution.py:329
  (54 shorter events, 2.7 us)
Async XLA Ops:
  2.8 14.7 %copy-start.1 = (bf16[1,64,128,64]{2,3,1,0:T(8,128)(2,1)S(1)}, bf16[1,64,128,64]{2,3,1,0:T(8,128)(2,1)}, u32[]{:S(2)}) copy-start(bf16[1,64,128,64]{2,3,1,0:T(8,128)(2,1)} %param.8) | copy-start | bytes 3145732
  2.9 9.2 %collective-permute-start = (bf16[8,64,128]{2,1,0:T(8,128)(2,1)S(1)}, bf16[8,64,128]{2,1,0:T(8,128)(2,1)S(1)}, u32[]{:S(2)}, u32[]{:S(2)}) collective-permute-start(bf16[8,64,128]{2,1,0:T(8,128)(2,1)S(1)} %get-tuple-element.14), channel_id=1, source_target_pairs={{0,2},{2,0},{4,6},{6,4},{8,10},{10,8},{12,14},{14,12},{1,3},{3,1},... | collective-permute-start | bytes 393224 | tf_op jit(solution)/shard_map/ppermute | solution.py:249
  5.9 6.6 %collective-permute-start.1 = (bf16[8,64,128]{2,1,0:T(8,128)(2,1)S(1)}, bf16[8,64,128]{2,1,0:T(8,128)(2,1)S(1)}, u32[]{:S(2)}, u32[]{:S(2)}) collective-permute-start(bf16[8,64,128]{2,1,0:T(8,128)(2,1)S(1)} %get-tuple-element.15), channel_id=1, source_target_pairs={{0,4},{2,6},{4,0},{6,2},{8,12},{10,14},{12,8},{14,10},{1,5},{3,7},... | collective-permute-start | bytes 393224 | tf_op jit(solution)/shard_map/ppermute | solution.py:249
  7.4 7.4 %collective-permute-start.2 = (bf16[8,64,128]{2,1,0:T(8,128)(2,1)S(1)}, bf16[8,64,128]{2,1,0:T(8,128)(2,1)S(1)}, u32[]{:S(2)}, u32[]{:S(2)}) collective-permute-start(bf16[8,64,128]{2,1,0:T(8,128)(2,1)S(1)} %get-tuple-element.16), channel_id=1, source_target_pairs={{0,6},{2,4},{4,2},{6,0},{8,14},{10,12},{12,10},{14,8},{1,7},{3,5},... | collective-permute-start | bytes 393224 | tf_op jit(solution)/shard_map/ppermute | solution.py:249
  7.6 3.6 %copy-start.8 = (bf16[64,64]{1,0:T(8,128)(2,1)S(1)}, bf16[64,64]{1,0:T(8,128)(2,1)}, u32[]{:S(2)}) copy-start(bf16[64,64]{1,0:T(8,128)(2,1)} %param.11) | copy-start | bytes 24580
  7.6 12.9 %collective-permute-start.7 = (bf16[8,64,128]{2,1,0:T(8,128)(2,1)S(1)}, bf16[8,64,128]{2,1,0:T(8,128)(2,1)S(1)}, u32[]{:S(2)}, u32[]{:S(2)}) collective-permute-start(bf16[8,64,128]{2,1,0:T(8,128)(2,1)S(1)} %get-tuple-element.18), channel_id=1, source_target_pairs={{0,2},{2,0},{4,6},{6,4},{8,10},{10,8},{12,14},{14,12},{1,3},{3,1},... | collective-permute-start | bytes 393224 | tf_op jit(solution)/shard_map/ppermute | solution.py:249
  9.6 11.0 %collective-permute-start.8 = (bf16[8,64,128]{2,1,0:T(8,128)(2,1)S(1)}, bf16[8,64,128]{2,1,0:T(8,128)(2,1)S(1)}, u32[]{:S(2)}, u32[]{:S(2)}) collective-permute-start(bf16[8,64,128]{2,1,0:T(8,128)(2,1)S(1)} %get-tuple-element.19), channel_id=1, source_target_pairs={{0,4},{2,6},{4,0},{6,2},{8,12},{10,14},{12,8},{14,10},{1,5},{3,7},... | collective-permute-start | bytes 393224 | tf_op jit(solution)/shard_map/ppermute | solution.py:249
  12.1 8.5 %collective-permute-start.9 = (bf16[8,64,128]{2,1,0:T(8,128)(2,1)S(1)}, bf16[8,64,128]{2,1,0:T(8,128)(2,1)S(1)}, u32[]{:S(2)}, u32[]{:S(2)}) collective-permute-start(bf16[8,64,128]{2,1,0:T(8,128)(2,1)S(1)} %get-tuple-element.20), channel_id=1, source_target_pairs={{0,6},{2,4},{4,2},{6,0},{8,14},{10,12},{12,10},{14,8},{1,7},{3,5},... | collective-permute-start | bytes 393224 | tf_op jit(solution)/shard_map/ppermute | solution.py:249
  14.9 8.5 %collective-permute-start.3 = (bf16[8,64,128]{2,1,0:T(8,128)(2,1)S(1)}, bf16[8,64,128]{2,1,0:T(8,128)(2,1)S(1)}, u32[]{:S(2)}, u32[]{:S(2)}) collective-permute-start(bf16[8,64,128]{2,1,0:T(8,128)(2,1)S(1)} %add_convert_fusion.3), channel_id=1, source_target_pairs={{0,8},{2,10},{4,12},{6,14},{8,0},{10,2},{12,4},{14,6},{1,9},{3,11}... | collective-permute-start | bytes 393224 | tf_op jit(solution)/shard_map/ppermute | solution.py:249
  17.5 5.6 %copy-start.2 = (bf16[3,2,3,3,64,64]{5,4,3,2,1,0:T(8,128)(2,1)S(1)}, bf16[3,2,3,3,64,64]{5,4,3,2,1,0:T(8,128)(2,1)}, u32[]{:S(2)}) copy-start(bf16[3,2,3,3,64,64]{5,4,3,2,1,0:T(8,128)(2,1)} %kernel_ref.1) | copy-start | bytes 1327108
  20.4 3.0 %collective-permute-start.15 = (f32[64,192]{1,0:T(8,128)S(1)}, f32[64,192]{1,0:T(8,128)S(1)}, u32[]{:S(2)}, u32[]{:S(2)}) collective-permute-start(f32[64,192]{1,0:T(8,128)S(1)} %sums.1.own_ref), channel_id=1, source_target_pairs={{0,1},{1,0},{2,3},{3,2},{4,5},{5,4},{6,7},{7,6},{8,9},{9,8},{10,11... | collective-permute-start | bytes 147464 | tf_op jit(solution)/shard_map/ppermute | solution.py:249
  20.6 13.9 %collective-permute-start.10 = (bf16[8,64,128]{2,1,0:T(8,128)(2,1)S(1)}, bf16[8,64,128]{2,1,0:T(8,128)(2,1)S(1)}, u32[]{:S(2)}, u32[]{:S(2)}) collective-permute-start(bf16[8,64,128]{2,1,0:T(8,128)(2,1)S(1)} %add_convert_fusion.1), channel_id=1, source_target_pairs={{0,8},{2,10},{4,12},{6,14},{8,0},{10,2},{12,4},{14,6},{1,9},{3,11}... | collective-permute-start | bytes 393224 | tf_op jit(solution)/shard_map/ppermute | solution.py:249
  23.6 19.2 %collective-permute-start.16 = (bf16[2,64,128]{2,1,0:T(8,128)(2,1)S(1)}, bf16[2,64,128]{2,1,0:T(8,128)(2,1)S(1)}, u32[]{:S(2)}, u32[]{:S(2)}) collective-permute-start(bf16[2,64,128]{2,1,0:T(8,128)(2,1)S(1)} %planes.1.refs_2_), channel_id=1, source_target_pairs={{0,4},{2,6},{4,8},{6,10},{8,12},{10,14},{1,5},{3,7},{5,9},{7,11},{... | collective-permute-start | bytes 98312 | tf_op jit(solution)/shard_map/ppermute | solution.py:255
  27.3 18.2 %collective-permute-start.17 = (bf16[2,64,128]{2,1,0:T(8,128)(2,1)S(1)}, bf16[2,64,128]{2,1,0:T(8,128)(2,1)S(1)}, u32[]{:S(2)}, u32[]{:S(2)}) collective-permute-start(bf16[2,64,128]{2,1,0:T(8,128)(2,1)S(1)} %planes.1.refs_2_), channel_id=1, source_target_pairs={{0,2},{2,4},{4,6},{6,8},{8,10},{10,12},{12,14},{1,3},{3,5},{5,7},{... | collective-permute-start | bytes 98312 | tf_op jit(solution)/shard_map/ppermute | solution.py:255
  31.2 6.2 %collective-permute-start.4 = (bf16[8,64,128]{2,1,0:T(8,128)(2,1)S(1)}, bf16[8,64,128]{2,1,0:T(8,128)(2,1)S(1)}, u32[]{:S(2)}, u32[]{:S(2)}) collective-permute-start(bf16[8,64,128]{2,1,0:T(8,128)(2,1)S(1)} %add_convert_fusion.2.after_ref.refs_0_), channel_id=1, source_target_pairs={{0,2},{2,0},{4,6},{6,4},{8,10},{10,8},{12,14},{14,12},{1,3},{3,1},... | collective-permute-start | bytes 393224 | tf_op jit(solution)/shard_map/ppermute | solution.py:249
  31.3 7.4 %collective-permute-start.5 = (bf16[8,64,128]{2,1,0:T(8,128)(2,1)S(1)}, bf16[8,64,128]{2,1,0:T(8,128)(2,1)S(1)}, u32[]{:S(2)}, u32[]{:S(2)}) collective-permute-start(bf16[8,64,128]{2,1,0:T(8,128)(2,1)S(1)} %add_convert_fusion.2.after_ref.refs_0_), channel_id=1, source_target_pairs={{0,4},{2,6},{4,0},{6,2},{8,12},{10,14},{12,8},{14,10},{1,5},{3,7},... | collective-permute-start | bytes 393224 | tf_op jit(solution)/shard_map/ppermute | solution.py:249
  34.6 6.3 %collective-permute-start.6 = (bf16[8,64,128]{2,1,0:T(8,128)(2,1)S(1)}, bf16[8,64,128]{2,1,0:T(8,128)(2,1)S(1)}, u32[]{:S(2)}, u32[]{:S(2)}) collective-permute-start(bf16[8,64,128]{2,1,0:T(8,128)(2,1)S(1)} %add_convert_fusion.2.after_ref.refs_0_), channel_id=1, source_target_pairs={{0,6},{2,4},{4,2},{6,0},{8,14},{10,12},{12,10},{14,8},{1,7},{3,5},... | collective-permute-start | bytes 393224 | tf_op jit(solution)/shard_map/ppermute | solution.py:249
  37.4 8.1 %collective-permute-start.18 = (bf16[2,64,128]{2,1,0:T(8,128)(2,1)S(1)}, bf16[2,64,128]{2,1,0:T(8,128)(2,1)S(1)}, u32[]{:S(2)}, u32[]{:S(2)}) collective-permute-start(bf16[2,64,128]{2,1,0:T(8,128)(2,1)S(1)} %planes.1.refs_2_), channel_id=1, source_target_pairs={{2,0},{4,2},{6,4},{8,6},{10,8},{12,10},{14,12},{3,1},{5,3},{7,5},{... | collective-permute-start | bytes 98312 | tf_op jit(solution)/shard_map/ppermute | solution.py:255
  38.7 6.9 %collective-permute-start.19 = (bf16[2,64,128]{2,1,0:T(8,128)(2,1)S(1)}, bf16[2,64,128]{2,1,0:T(8,128)(2,1)S(1)}, u32[]{:S(2)}, u32[]{:S(2)}) collective-permute-start(bf16[2,64,128]{2,1,0:T(8,128)(2,1)S(1)} %planes.1.refs_2_), channel_id=1, source_target_pairs={{4,0},{6,2},{8,4},{10,6},{12,8},{14,10},{5,1},{7,3},{9,5},{11,7},{... | collective-permute-start | bytes 98312 | tf_op jit(solution)/shard_map/ppermute | solution.py:255
  40.8 5.8 %collective-permute-start.11 = (bf16[8,64,128]{2,1,0:T(8,128)(2,1)S(1)}, bf16[8,64,128]{2,1,0:T(8,128)(2,1)S(1)}, u32[]{:S(2)}, u32[]{:S(2)}) collective-permute-start(bf16[8,64,128]{2,1,0:T(8,128)(2,1)S(1)} %add_convert_fusion.refs_6_.refs_4_), channel_id=1, source_target_pairs={{0,2},{2,0},{4,6},{6,4},{8,10},{10,8},{12,14},{14,12},{1,3},{3,1},... | collective-permute-start | bytes 393224 | tf_op jit(solution)/shard_map/ppermute | solution.py:249
  42.8 5.7 %collective-permute-start.12 = (bf16[8,64,128]{2,1,0:T(8,128)(2,1)S(1)}, bf16[8,64,128]{2,1,0:T(8,128)(2,1)S(1)}, u32[]{:S(2)}, u32[]{:S(2)}) collective-permute-start(bf16[8,64,128]{2,1,0:T(8,128)(2,1)S(1)} %add_convert_fusion.refs_6_.refs_4_), channel_id=1, source_target_pairs={{0,4},{2,6},{4,0},{6,2},{8,12},{10,14},{12,8},{14,10},{1,5},{3,7},... | collective-permute-start | bytes 393224 | tf_op jit(solution)/shard_map/ppermute | solution.py:249
  45.5 5.9 %collective-permute-start.13 = (bf16[8,64,128]{2,1,0:T(8,128)(2,1)S(1)}, bf16[8,64,128]{2,1,0:T(8,128)(2,1)S(1)}, u32[]{:S(2)}, u32[]{:S(2)}) collective-permute-start(bf16[8,64,128]{2,1,0:T(8,128)(2,1)S(1)} %add_convert_fusion.refs_6_.refs_4_), channel_id=1, source_target_pairs={{0,6},{2,4},{4,2},{6,0},{8,14},{10,12},{12,10},{14,8},{1,7},{3,5},... | collective-permute-start | bytes 393224 | tf_op jit(solution)/shard_map/ppermute | solution.py:249
  45.5 5.9 %collective-permute-start.14 = (bf16[2,64,128]{2,1,0:T(8,128)(2,1)S(1)}, bf16[2,64,128]{2,1,0:T(8,128)(2,1)S(1)}, u32[]{:S(2)}, u32[]{:S(2)}) collective-permute-start(bf16[2,64,128]{2,1,0:T(8,128)(2,1)S(1)} %slice_select_fusion), channel_id=1, source_target_pairs={{0,1},{1,0},{2,3},{3,2},{4,5},{5,4},{6,7},{7,6},{8,9},{9,8},{10,11... | collective-permute-start | bytes 98312 | tf_op jit(solution)/shard_map/ppermute | solution.py:249
  45.7 5.7 %copy-start.6 = (bf16[128,64]{0,1:T(8,128)(2,1)S(1)}, bf16[128,64]{0,1:T(8,128)(2,1)}, u32[]{:S(2)}) copy-start(bf16[128,64]{0,1:T(8,128)(2,1)} %param.15) | copy-start | bytes 49156
  (6 other events, 8.8 us)

commit v2 on v1

--- a/solution.py
+++ b/solution.py
@@ -127,18 +127,41 @@
     return lax.axis_index("gx") % 4, lax.axis_index("gy")
 
 
-def front_kernel(row_ref, vox_ref, occ_ref, *out_refs, chunk):
-    rows, c, z = vox_ref.shape
+def weighted(vox, occ, row_ref, out_ref):
+    weight = jnp.broadcast_to(row_ref[...].astype(f32), vox.shape[:0:-1]).T
+    occ = occ.astype(f32)
+    for i in range(vox.shape[0]):
+        out_ref[i] = (vox[i].astype(f32) * occ[i : i + 1] * weight).astype(out_ref.dtype)
+
+
+def quarter_at(rows, chunk, d):
     low, core = place()
-    base = chunk_base(chunk, core, rows)
     quarter = rows // 8
-    weight = row_ref[...].astype(f32)
+    return pl.multiple_of(chunk_base(chunk, core, rows) + jnp.bitwise_xor(low, d) * quarter, quarter)
+
+
+def fetch_kernel(row_hbm, vox_hbm, occ_hbm, *refs):
+    out_refs, (row_ref, vox_ref, occ_ref, row_sem, vox_sem, occ_sem) = refs[:4], refs[4:]
+    rows = vox_hbm.shape[0]
+    quarter = rows // 8
+    copies = [pltpu.make_async_copy(row_hbm, row_ref, row_sem)]
     for d in (1, 2, 3, 0):
-        first = base + jnp.bitwise_xor(low, d) * quarter
-        occ = occ_ref[pl.ds(first, quarter)].astype(f32)
-        for i in range(quarter):
-            value = vox_ref[first + i].astype(f32) * occ[i : i + 1] * weight
-            out_refs[d][i] = value.astype(out_refs[d].dtype)
+        part = pl.ds(quarter_at(rows, 0, d), quarter)
+        copies.append(pltpu.make_async_copy(vox_hbm.at[part], vox_ref.at[d], vox_sem.at[d]))
+        copies.append(pltpu.make_async_copy(occ_hbm.at[part], occ_ref.at[d], occ_sem.at[d]))
+    for copy in copies:
+        copy.start()
+    for copy in copies:
+        copy.wait()
+    for d in (1, 2, 3, 0):
+        weighted(vox_ref[d], occ_ref[d], row_ref, out_refs[d])
+
+
+def front_kernel(row_ref, vox_ref, occ_ref, *out_refs):
+    rows = vox_ref.shape[0]
+    for d in (1, 2, 3, 0):
+        part = pl.ds(quarter_at(rows, 1, d), rows // 8)
+        weighted(vox_ref[part], occ_ref[part], row_ref, out_refs[d])
 
 
 def chunk_base(chunk, core, rows):
@@ -150,38 +173,73 @@
     del after_ref
     rows, c, z = vox_ref.shape
     depth = depth_ref[...].astype(f32)
-    column = column_ref[...].astype(f32)
-    lane = lax.broadcasted_iota(jnp.int32, (c, rows), 1)
+    columns = column_ref[...].astype(f32).T
+    at = lax.broadcasted_iota(jnp.int32, (c, z), 1) % rows
+    ones = jnp.ones((2 * z, z), bf16)
     xz = jnp.zeros((c, z), f32)
-    xy = jnp.zeros((c, rows), f32)
-    for y in range(rows):
-        feats = vox_ref[y].astype(f32) * occ_ref[y : y + 1].astype(f32)
-        xz = xz + feats * column[:, y : y + 1]
-        xy = jnp.where(lane == y, jnp.sum(feats * depth, axis=1, keepdims=True), xy)
+    xy = jnp.zeros((c, z), f32)
+    group = 8
+    for base in range(0, rows, group):
+        terms = []
+        for y in range(base, base + group):
+            feats = vox_ref[y].astype(f32) * occ_ref[y : y + 1].astype(f32)
+            xz = xz + feats * columns[:, y : y + 1]
+            term = feats * depth
+            high = term.astype(bf16)
+            terms.append(jnp.concatenate([high, (term - high.astype(f32)).astype(bf16)], axis=1))
+        total = jnp.dot(jnp.concatenate(terms, axis=0), ones, preferred_element_type=f32)
+        for i in range(group):
+            xy = jnp.where(at == base + i, total[i * c : (i + 1) * c], xy)
     out_ref[:, :z] = xz
     out_ref[:, z:] = xy.astype(bf16).astype(f32)
 
 
-def planes_kernel(own_ref, other_ref, after_ref, out_ref):
+def merge_kernel(own_ref, first_ref, second_ref, third_ref, message_ref, other_ref, out_ref):
+    quarter, c, z = own_ref.shape
+    for i in range(quarter):
+        total = own_ref[i] + first_ref[i].astype(f32) + second_ref[i].astype(f32) + third_ref[i].astype(f32)
+        out_ref[i] = total.astype(bf16)
+    _, core = place()
+    lane = lax.broadcasted_iota(jnp.int32, (c, z), 1)
+    here = (lane < z // 2) == (core == 0)
+    out_ref[quarter] = jnp.where(here, message_ref[:, z:], other_ref[:, z:]).astype(bf16)
+    out_ref[quarter + 1] = (message_ref[:, :z] + other_ref[:, :z]).astype(bf16)
+
+
+def add_kernel(first_ref, second_ref, after_ref, out_ref):
     del after_ref
-    z = out_ref.shape[2]
-    _, core = place()
-    own, other = own_ref[...], other_ref[...]
-    own_xy, other_xy = own[:, z:], other[:, z:]
-    first = jnp.where(core == 0, own_xy, other_xy)
-    second = jnp.where(core == 0, other_xy, own_xy)
-    out_ref[0] = jnp.concatenate([first, second], axis=1).astype(bf16)
-    out_ref[1] = (own[:, :z] + other[:, :z]).astype(bf16)
-
-
-def weights_kernel(kernel_ref, after_ref, out_ref):
+    out_ref[...] = (first_ref[...].astype(f32) + second_ref[...].astype(f32)).astype(bf16)
+
+
+def join_kernel(sent_ref, got_ref, first_ref, second_ref, third_ref):
+    quarter = sent_ref.shape[0] - 2
+    for i in range(quarter):
+        total = (sent_ref[i].astype(f32) + got_ref[i].astype(f32)).astype(bf16)
+        for ref in (first_ref, second_ref, third_ref):
+            ref[i] = total
+    at = lax.axis_index("gx")
+    odd = (at // 2 + at) % 2 == 1
+    for p in range(2):
+        own, far = sent_ref[quarter + p], got_ref[quarter + p]
+        first_ref[quarter + p] = own
+        second_ref[quarter + p] = own
+        second_ref[quarter + 2 + p] = far
+        third_ref[quarter + p] = jnp.where(odd, own.astype(f32), far.astype(f32)).astype(bf16)
+
+
+def weights_kernel(kernel_ref, expand_ref, after_ref, small_ref, main_ref, expanded_ref):
     del after_ref
+    expanded_ref[...] = expand_ref[...].astype(f32).T.astype(bf16)
     for p in range(kernel_ref.shape[0]):
         for l in range(kernel_ref.shape[1]):
             for a in range(3):
                 rows = jnp.concatenate([kernel_ref[p, l, a, b] for b in range(3)], axis=0)
                 o = rows.shape[1]
-                out_ref[p, l, a * o : (a + 1) * o] = rows.astype(f32).T.astype(bf16)
+                value = rows.astype(f32).T.astype(bf16)
+                if p < 2:
+                    small_ref[p, l, a * o : (a + 1) * o] = value
+                else:
+                    main_ref[l, a * o : (a + 1) * o] = value
 
 
 def small_kernel(*refs, last):
@@ -200,49 +258,73 @@
         out_ref[p] = value.astype(bf16)
 
 
-def main_kernel(*refs, group):
-    pieces, (halo_ref, vox_ref, occ_ref, small_ref, weight_ref, expand_ref, shrink_ref) = refs[:8], refs[8:15]
-    out_ref, plane_ref, inner_ref = refs[15:]
-    rows, c, z = vox_ref.shape
-    low, core = place()
-    quarter = rows // 8
-    top = jnp.where(core == 0, 0.0, 1.0)
-    bottom = 1.0 - top
-    halo = halo_ref[...].astype(f32)
-    plane_ref[0:2] = (halo * top).astype(bf16)
-    plane_ref[rows + 2 : rows + 4] = (halo * bottom).astype(bf16)
-    for chunk in range(2):
-        for d in range(4):
-            first = 2 + chunk_base(chunk, core, rows) + jnp.bitwise_xor(low, d) * quarter
-            plane_ref[pl.ds(first, quarter)] = pieces[4 * chunk + d][...]
-    in_group = (rows + 2) // 3 if (rows + 2) % 3 == 0 else rows + 2
-    for g in range((rows + 2) // in_group):
-        base = g * in_group
-        outs = conv_rows(plane_ref[base : base + in_group + 2], weight_ref[0])
-        for i, v in enumerate(outs):
+def block(rows_ref, inner_ref, masks, first, count, operands, stage_ref, out_hbm, sem):
+    vox_ref, occ_ref, small_ref, weight_ref, expand_ref, shrink_ref = operands
+    z = vox_ref.shape[2]
+    inside = (count + 2) // 2
+    for base in (0, inside):
+        for i, v in enumerate(conv_rows(rows_ref[base : base + inside + 2], weight_ref[0])):
             v = silu(v)
-            if base + i == 0:
-                v = v * top
-            if base + i == rows + 1:
-                v = v * bottom
+            if base + i in masks:
+                v = v * masks[base + i]
             inner_ref[base + i] = v.astype(bf16)
     xz = small_ref[1].astype(f32)
     xy = small_ref[0].astype(f32)
-    for g in range(rows // group):
-        base = g * group
-        outs = conv_rows(inner_ref[base : base + group + 2], weight_ref[1])
+    start, other = first
+    _, core = place()
+    lanes = lambda by: pltpu.roll(xy, z - by, 1) if by else xy
+    xy = jnp.where(core == 0, lanes(start), lanes(other))
+    first = jnp.where(core == 0, start, other)
+    group = count // 2
+    copies = []
+    for base in (0, group):
         mixed = []
-        for i, v in enumerate(outs):
-            y = base + i
-            product = xy[:, y : y + 1] * xz * v.astype(bf16).astype(f32)
+        for i, v in enumerate(conv_rows(inner_ref[base : base + group + 2], weight_ref[1])):
+            product = xy[:, base + i : base + i + 1] * xz * v.astype(bf16).astype(f32)
             mixed.append((product_scale * product).astype(bf16))
         mixed = jnp.concatenate(mixed, axis=1)
         hidden = silu(jnp.dot(expand_ref[...], mixed, preferred_element_type=f32)).astype(bf16)
         branch = jnp.dot(shrink_ref[...], hidden, preferred_element_type=f32)
         for i in range(group):
-            y = base + i
-            feats = vox_ref[y].astype(f32) * occ_ref[y : y + 1].astype(f32)
-            out_ref[y] = (feats + branch[:, i * z : (i + 1) * z]).astype(bf16)
+            y = first + base + i
+            feats = vox_ref[y].astype(f32) * occ_ref[pl.ds(y, 1)].astype(f32)
+            stage_ref[base + i] = (feats + branch[:, i * z : (i + 1) * z]).astype(bf16)
+        part = pl.ds(base, group)
+        copies.append(
+            pltpu.make_async_copy(stage_ref.at[part], out_hbm.at[pl.ds(first + base, group)], sem.at[base // group])
+        )
+        copies[-1].start()
+    for copy in copies:
+        copy.wait()
+
+
+def near_kernel(*refs):
+    pieces, halo_ref, operands = refs[:4], refs[4], refs[5:11]
+    out_hbm, edge_ref, rows_ref, inner_ref, stage_ref, sem = refs[11:]
+    rows = operands[0].shape[0]
+    quarter, half = rows // 8, rows // 2
+    low, core = place()
+    rows_ref[pl.ds(jnp.where(core == 0, half, 0), 2)] = halo_ref[...]
+    for d in range(4):
+        at = jnp.where(core == 0, 0, 2) + jnp.bitwise_xor(low, d) * quarter
+        rows_ref[pl.ds(at, quarter)] = pieces[d][0:quarter]
+    edge_ref[...] = rows_ref[pl.ds(jnp.where(core == 0, 0, half - 2), 4)]
+    block(rows_ref, inner_ref, {}, (half + 2, 0), half - 2, operands, stage_ref, out_hbm, sem)
+
+
+def rest_kernel(*refs):
+    pieces, edge_ref, operands = refs[:4], refs[4], refs[5:11]
+    _, out_hbm, rows_ref, inner_ref, stage_ref, sem = refs[11:]
+    rows, c, z = operands[0].shape
+    quarter, half = rows // 8, rows // 2
+    low, core = place()
+    rows_ref[pl.ds(jnp.where(core == 0, 0, half + 4), 2)] = jnp.zeros((2, c, z), bf16)
+    rows_ref[pl.ds(jnp.where(core == 0, half + 2, 0), 4)] = edge_ref[...]
+    for d in range(4):
+        at = jnp.where(core == 0, 2, 4) + jnp.bitwise_xor(low, d) * quarter
+        rows_ref[pl.ds(at, quarter)] = pieces[d][...]
+    masks = {0: jnp.where(core == 0, 0.0, 1.0), half + 3: jnp.where(core == 0, 1.0, 0.0)}
+    block(rows_ref, inner_ref, masks, (0, half - 2), half + 2, operands, stage_ref, out_hbm, sem)
 
 
 def swap(value, axis, bit):
@@ -263,14 +345,14 @@
     return pl.BlockSpec(memory_space=pl.ANY)
 
 
-def call(kernel, name, out_shape, specs, scratch=()):
+def call(kernel, name, out_shape, specs, scratch=(), mib=40):
     return pl.pallas_call(
         kernel,
         out_shape=out_shape,
         in_specs=specs,
         out_specs=jax.tree.map(lambda _: vmem(), out_shape),
         scratch_shapes=list(scratch),
-        compiler_params=pltpu.CompilerParams(vmem_limit_bytes=40 * 1024 * 1024),
+        compiler_params=pltpu.CompilerParams(vmem_limit_bytes=mib * 1024 * 1024),
         name=name,
     )
 
@@ -283,56 +365,108 @@
     rows, c, z = vox.shape
     low, core = place()
     quarter = rows // 8
-    gx_size = lax.axis_size("gx")
-
-    row_column = jnp.broadcast_to(row_weights[0][:, None], (c, z))
-    piece = lambda kind: jax.ShapeDtypeStruct((quarter, c, z), kind)
-    totals, arrived = [], []
-    for chunk in range(2):
-        own, *send = call(
-            functools.partial(front_kernel, chunk=chunk), f"front{chunk}", [piece(f32)] + [piece(bf16)] * 3, [vmem()] * 3
-        )(row_column, vox, occ)
-        got = [swap(value, "gx", d) for d, value in zip((1, 2, 3), send)]
-        arrived.append(got)
-        totals.append((own + got[0].astype(f32) + got[1].astype(f32) + got[2].astype(f32)).astype(bf16))
-    bit = 4
-    while bit < gx_size:
-        totals = [(t.astype(f32) + swap(t, "gx", bit).astype(f32)).astype(bf16) for t in totals]
-        bit *= 2
-    pieces = [[t] + [swap(t, "gx", d) for d in (1, 2, 3)] for t in totals]
-    edge = jnp.bitwise_xor(low, jnp.where(core == 0, 3, 0))
-    beside = pieces[0][0]
-    for d in (1, 2, 3):
-        beside = jnp.where(edge == d, pieces[0][d], beside)
-    halo = swap(jnp.where(core == 0, beside[quarter - 2 :], beside[:2]), "gy", 1)
+    gx_size, gx = lax.axis_size("gx"), lax.axis_index("gx")
+
+    piece = lambda kind, n=quarter: jax.ShapeDtypeStruct((n, c, z), kind)
+    shapes = [piece(f32)] + [piece(bf16)] * 3
+    scratch = [
+        pltpu.VMEM(row_weights.shape, bf16),
+        pltpu.VMEM((4, quarter, c, z), bf16),
+        pltpu.VMEM((4, quarter, z), jnp.int32),
+        pltpu.SemaphoreType.DMA,
+        pltpu.SemaphoreType.DMA((4,)),
+        pltpu.SemaphoreType.DMA((4,)),
+    ]
+    hbm = pl.BlockSpec(memory_space=pltpu.HBM)
+    inputs = row_weights, vox, occ
+    fronts = call(fetch_kernel, "fetch", shapes, [hbm] * 3, scratch, mib=62)(*inputs)
+    fronts += call(front_kernel, "front", shapes, [vmem()] * 3)(*inputs)
+    owns = [fronts[0], fronts[4]]
+    gots = [[swap(fronts[4 * chunk + d], "gx", d) for d in (1, 2, 3)] for chunk in range(2)]
 
     message = call(
-        sums_kernel, "sums", jax.ShapeDtypeStruct((c, z + rows), f32), [vmem()] * 4 + [anywhere()]
-    )(vox, occ, column_weights.T, depth_weights.T, arrived[0][0])
-    weights = call(
+        sums_kernel, "sums", jax.ShapeDtypeStruct((c, 2 * z), f32), [vmem()] * 4 + [anywhere()]
+    )(vox, occ, column_weights, depth_weights.T, gots[0][0])
+    stacked = plane_kernels.shape[1:2] + (3 * c, 3 * c)
+    small_weights, main_weights, expanded = call(
         weights_kernel,
         "weights",
-        jax.ShapeDtypeStruct(plane_kernels.shape[:2] + (3 * c, 3 * c), bf16),
-        [vmem(), anywhere()],
-    )(plane_kernels, arrived[0][1])
-    planes = call(
-        planes_kernel, "planes", jax.ShapeDtypeStruct((2, c, z), bf16), [vmem()] * 2 + [anywhere()]
-    )(message, swap(message, "gy", 1), totals[0])
-    near = [shifted(planes, "gx", by) if by else planes for by in (-2, -1, 0, 1, 2)]
+        [
+            jax.ShapeDtypeStruct((2,) + stacked, bf16),
+            jax.ShapeDtypeStruct(stacked, bf16),
+            jax.ShapeDtypeStruct(expand_weight.shape[::-1], bf16),
+        ],
+        [vmem()] * 2 + [anywhere()],
+    )(plane_kernels, expand_weight, gots[1][0])
+    merged = call(merge_kernel, "merge", piece(bf16, quarter + 2), [vmem()] * 6)(
+        owns[0], *gots[0], message, swap(message, "gy", 1)
+    )
+    second = owns[1]
+    for got in gots[1]:
+        second = second + got.astype(f32)
+    second = second.astype(bf16)
+    add = lambda value, bit: (value.astype(f32) + swap(value, "gx", bit).astype(f32)).astype(bf16)
+    planes = merged[quarter:]
+    if gx_size == 8:
+        sent = call(
+            join_kernel, "join", [piece(bf16, quarter + n) for n in (2, 4, 2)], [vmem()] * 2
+        )(merged, swap(merged, "gx", 4))
+        got = [swap(value, "gx", d) for d, value in zip((1, 2, 3), sent)]
+        second = call(add_kernel, "add", piece(bf16), [vmem()] * 2 + [anywhere()])(second, swap(second, "gx", 4), got[2])
+        pieces = [[sent[0]] + got, None]
+        one, two, three = (value[quarter:] for value in got)
+        odd, right = gx // 2 % 2 == 1, gx % 2 == 1
+        keep = lambda inside, value: jnp.where(inside, value, jnp.zeros_like(value))
+        near = [
+            keep(gx >= 2, jnp.where(odd, two[:2], two[2:])),
+            keep(gx >= 1, jnp.where(right, one, three)),
+            planes,
+            keep(gx < gx_size - 1, jnp.where(right, three, one)),
+            keep(gx < gx_size - 2, jnp.where(odd, two[2:], two[:2])),
+        ]
+    else:
+        first, bit = merged[:quarter], 4
+        while bit < gx_size:
+            first, second = add(first, bit), add(second, bit)
+            bit *= 2
+        pieces = [[first] + [swap(first, "gx", d) for d in (1, 2, 3)], None]
+        near = [shifted(planes, "gx", by) if by else planes for by in (-2, -1, 0, 1, 2)]
+    pieces[1] = [second] + [swap(second, "gx", d) for d in (1, 2, 3)]
+    edge = jnp.bitwise_xor(low, jnp.where(core == 0, 3, 0))
+    beside = pieces[0][0][:quarter]
+    for d in (1, 2, 3):
+        beside = jnp.where(edge == d, pieces[0][d][:quarter], beside)
+    halo = swap(jnp.where(core == 0, beside[quarter - 2 :], beside[:2]), "gy", 1)
+
     small = call(
         functools.partial(small_kernel, last=gx_size - 1),
         "small",
         jax.ShapeDtypeStruct(planes.shape, bf16),
         [vmem()] * 6 + [anywhere()],
-    )(*near, weights[:2], totals[1])
-
-    out = call(
-        functools.partial(main_kernel, group=16),
-        "block",
-        jax.ShapeDtypeStruct((rows, c, z), bf16),
-        [vmem()] * 15,
-        [pltpu.VMEM((rows + 4, c, z), bf16), pltpu.VMEM((rows + 2, c, z), bf16)],
-    )(*pieces[0], *pieces[1], halo, vox, occ, small, weights[2], expand_weight.T, shrink_weight.T)
+    )(*near, small_weights, second)
+
+    operands = vox, occ, small, main_weights, expanded, shrink_weight.T
+    whole = jax.ShapeDtypeStruct((rows, c, z), bf16)
+    half = rows // 2
+    out, edge = pl.pallas_call(
+        near_kernel,
+        out_shape=[whole, piece(bf16, 4)],
+        in_specs=[vmem()] * 11,
+        out_specs=[hbm, vmem()],
+        scratch_shapes=[pltpu.VMEM((n, c, z), bf16) for n in (half + 2, half, half - 2)] + [pltpu.SemaphoreType.DMA((2,))],
+        compiler_params=pltpu.CompilerParams(vmem_limit_bytes=40 * 1024 * 1024),
+        name="near",
+    )(*pieces[0], halo, *operands)
+    out = pl.pallas_call(
+        rest_kernel,
+        out_shape=whole,
+        in_specs=[vmem()] * 11 + [hbm],
+        out_specs=hbm,
+        scratch_shapes=[pltpu.VMEM((n, c, z), bf16) for n in (half + 6, half + 4, half + 2)] + [pltpu.SemaphoreType.DMA((2,))],
+        input_output_aliases={11: 0},
+        compiler_params=pltpu.CompilerParams(vmem_limit_bytes=40 * 1024 * 1024),
+        name="rest",
+    )(*pieces[1], edge, *operands, out)
     return out[None].transpose(0, 1, 3, 2)
 
 
@@ -352,7 +486,7 @@
     def whole(voxels, *rest):
         gx, gy = mesh.shape["gx"], mesh.shape["gy"]
         x, y, z = voxels.shape[0] // mesh.shape["groups"], voxels.shape[1], voxels.shape[2]
-        fits = gy == 2 and gx >= 4 and gx & (gx - 1) == 0 and x == gx and y == z and z == 128 and y % 32 == 0
+        fits = gy == 2 and gx >= 4 and gx & (gx - 1) == 0 and x == gx and y == z and z == 128
         part = shards if fits else general
         mapped = jax.shard_map(part, mesh=mesh, in_specs=in_specs, out_specs=out_specs, check_vma=False)
         return mapped(voxels, *rest)

time: 56.9 us -> 48.3 us (0.85)
  starting transfers between devices: 32.1 us -> 20 us
  waiting for transfers between devices: 10.6 us -> 14.3 us
  local copies, waits for them, and re-layouts: 3.68 us -> 2.18 us
  Pallas kernels: 9.54 us -> 11 us
    ppermute x4 -> x0, starting transfers between devices: 10.2 us -> none  [shifted(): return lax.ppermute(value, axis, pairs)]
    ppermute x16, waiting for transfers between devices: 10.6 us -> 14.3 us  [swap(): lax.ppermute(value, axis, [(i, i ^ bit) for i in range(lax.axis_size(axis...]
    ppermute x16, starting transfers between devices: 22 us -> 20 us  [swap(): lax.ppermute(value, axis, [(i, i ^ bit) for i in range(lax.axis_size(axis...]
    pallas_call x6 -> x9, Pallas kernels: 8.61 us -> 10.1 us  [the longest x1 2.94 us: shards(): pl.pallas_call(rest_kernel, out_shape=whole, in_specs=[vmem()] * 11 + [hb...]
    unnamed x22 -> x18, local copies, waits for them, and re-layouts: 3.57 us -> 2.18 us
  transfers between devices with their start and end apart: 20 -> 16, of which waited for: 5 -> 8; matrix products, arithmetic and copies ran while one was open for 1% -> 0% of each run, Pallas kernels for 8% -> 12%
where the time goes in v2:
time: 48.3 us; the launch traced here: 47.8 us
  starting transfers between devices  20 us (41%)
  waiting for transfers between devices  14.3 us (30%)
  Pallas kernels  11 us (23%)
  local copies, waits for them, and re-layouts  2.18 us (5%)
    ppermute x16, starting transfers between devices, swap(): lax.ppermute(value, axis, [(i, i ^ bit) for i in range(lax.axis_size(axis...  20 us
    ppermute x16, waiting for transfers between devices, swap(): lax.ppermute(value, axis, [(i, i ^ bit) for i in range(lax.axis_size(axis...  14.3 us
    pallas_call x1, Pallas kernels, shards(): pl.pallas_call(rest_kernel, out_shape=whole, in_specs=[vmem()] * 11 + [hb...  2.94 us
    pallas_call x1, Pallas kernels, shards(): pl.pallas_call(near_kernel, out_shape=[whole, piece(bf16, 4)], in_specs=[...  2.72 us
    pallas_call x1, Pallas kernels, shards(): call(fetch_kernel, 'fetch', shapes, [hbm] * 3, scratch, mib=62)(*inputs)  2.25 us
    unnamed x18, local copies, waits for them, and re-layouts  2.18 us
  transfers between devices with their start and end apart: 16, of which 8 were waited for; matrix products, arithmetic and copies ran while one was open for 0% of the time, Pallas kernels for 12%

profile of v2, /device:TPU:0, one launch (start us, length us, event | category | flops | bytes accessed | tf_op | source)
XLA Modules:
  0.0 47.8 jit_solution(2946311907852891505)
XLA Ops:
  0.0 2.3 %fetch.1 = (f32[8,64,128]{2,1,0:T(8,128)}, bf16[8,64,128]{2,1,0:T(8,128)(2,1)}, bf16[8,64,128]{2,1,0:T(8,128)(2,1)}, bf16[8,64,128]{2,1,0:T(8,128)(2,1)}) custom-call(bf16[1,64]{1,0:T(2,128)(2,1)} %row_hbm.1, bf16[64,64,128]{2,1,0:T(8,128)(2,1)} %bitcast.9, s32[64,128]{1,0:T(8,128)} %bitcast.14), custom_call_target="tpu_custom_call" | custom-call | tf_op jit(solution)/shard_map/fetch/pallas_call | solution.py:382
  2.3 3.0 %collective-permute-start.4 = (bf16[8,64,128]{2,1,0:T(8,128)(2,1)}, bf16[8,64,128]{2,1,0:T(8,128)(2,1)S(1)}, u32[]{:S(2)}, u32[]{:S(2)}) collective-permute-start(bf16[8,64,128]{2,1,0:T(8,128)(2,1)} %get-tuple-element.26), channel_id=1, source_target_pairs={{0,2},{2,0},{4,6},{6,4},{8,10},{10,8},{12,14},{14,12},{1,3},{3,1},... | collective-permute-start | bytes 393224 | tf_op jit(solution)/shard_map/ppermute | solution.py:331
  5.3 1.6 %collective-permute-start.5 = (bf16[8,64,128]{2,1,0:T(8,128)(2,1)}, bf16[8,64,128]{2,1,0:T(8,128)(2,1)S(1)}, u32[]{:S(2)}, u32[]{:S(2)}) collective-permute-start(bf16[8,64,128]{2,1,0:T(8,128)(2,1)} %get-tuple-element.27), channel_id=1, source_target_pairs={{0,4},{2,6},{4,0},{6,2},{8,12},{10,14},{12,8},{14,10},{1,5},{3,7},... | collective-permute-start | bytes 393224 | tf_op jit(solution)/shard_map/ppermute | solution.py:331
  6.9 2.1 %collective-permute-done.4.after_ref.first_ref = bf16[8,64,128]{2,1,0:T(8,128)(2,1)S(1)} collective-permute-done((bf16[8,64,128]{2,1,0:T(8,128)(2,1)}, bf16[8,64,128]{2,1,0:T(8,128)(2,1)S(1)}, u32[]{:S(2)}, u32[]{:S(2)}) %collective-permute-start.4) | collective-permute-done | bytes 131104 | tf_op jit(solution)/shard_map/ppermute | solution.py:331
  9.0 0.7 %copy-done.5 = bf16[64,64]{1,0:T(8,128)(2,1)S(1)} copy-done((bf16[64,64]{1,0:T(8,128)(2,1)S(1)}, bf16[64,64]{1,0:T(8,128)(2,1)}, u32[]{:S(2)}) %copy-start.5) | copy-done | bytes 8216
  9.7 0.7 %copy-done.6 = bf16[128,64]{0,1:T(8,128)(2,1)S(1)} copy-done((bf16[128,64]{0,1:T(8,128)(2,1)S(1)}, bf16[128,64]{0,1:T(8,128)(2,1)}, u32[]{:S(2)}) %copy-start.6) | copy-done | bytes 16408
  10.4 0.9 %sums.1.message_ref = f32[64,256]{1,0:T(8,128)S(1)} custom-call(bf16[64,64,128]{2,1,0:T(8,128)(2,1)S(1)} %bitcast.10, s32[64,128]{1,0:T(8,128)S(1)} %bitcast.15, bf16[64,64]{1,0:T(8,128)(2,1)S(1)} %copy-done.5, bf16[64,128]{1,0:T(8,128)(2,1)S(1)} %bitcast.21, bf16[8,64,128]{2,1,0:T(8,128)(2,1)S(1)} %collective-permute-done.4.after_ref.first_ref), custom_call_target="tpu_custom_call" | custom-call | tf_op jit(solution)/shard_map/sums/pallas_call | solution.py:387
  11.8 1.2 %collective-permute-done.6.third_ref = bf16[8,64,128]{2,1,0:T(8,128)(2,1)S(1)} collective-permute-done((bf16[8,64,128]{2,1,0:T(8,128)(2,1)}, bf16[8,64,128]{2,1,0:T(8,128)(2,1)S(1)}, u32[]{:S(2)}, u32[]{:S(2)}) %collective-permute-start.6) | collective-permute-done | bytes 131104 | tf_op jit(solution)/shard_map/ppermute | solution.py:331
  13.1 2.8 %collective-permute-start.8 = (bf16[10,64,128]{2,1,0:T(8,128)(2,1)S(1)}, bf16[10,64,128]{2,1,0:T(8,128)(2,1)S(1)}, u32[]{:S(2)}, u32[]{:S(2)}) collective-permute-start(bf16[10,64,128]{2,1,0:T(8,128)(2,1)S(1)} %merge.1.sent_ref), channel_id=1, source_target_pairs={{0,8},{2,10},{4,12},{6,14},{8,0},{10,2},{12,4},{14,6},{1,9},{3,11}... | collective-permute-start | bytes 491528 | tf_op jit(solution)/shard_map/ppermute | solution.py:331
  16.2 1.5 %collective-permute-start = (bf16[8,64,128]{2,1,0:T(8,128)(2,1)S(1)}, bf16[8,64,128]{2,1,0:T(8,128)(2,1)S(1)}, u32[]{:S(2)}, u32[]{:S(2)}) collective-permute-start(bf16[8,64,128]{2,1,0:T(8,128)(2,1)S(1)} %get-tuple-element.22), channel_id=1, source_target_pairs={{0,2},{2,0},{4,6},{6,4},{8,10},{10,8},{12,14},{14,12},{1,3},{3,1},... | collective-permute-start | bytes 393224 | tf_op jit(solution)/shard_map/ppermute | solution.py:331
  17.7 1.6 %collective-permute-start.1 = (bf16[8,64,128]{2,1,0:T(8,128)(2,1)S(1)}, bf16[8,64,128]{2,1,0:T(8,128)(2,1)S(1)}, u32[]{:S(2)}, u32[]{:S(2)}) collective-permute-start(bf16[8,64,128]{2,1,0:T(8,128)(2,1)S(1)} %get-tuple-element.23), channel_id=1, source_target_pairs={{0,4},{2,6},{4,0},{6,2},{8,12},{10,14},{12,8},{14,10},{1,5},{3,7},... | collective-permute-start | bytes 393224 | tf_op jit(solution)/shard_map/ppermute | solution.py:331
  19.7 4.0 %collective-permute-done.8.got_ref = bf16[10,64,128]{2,1,0:T(8,128)(2,1)S(1)} collective-permute-done((bf16[10,64,128]{2,1,0:T(8,128)(2,1)S(1)}, bf16[10,64,128]{2,1,0:T(8,128)(2,1)S(1)}, u32[]{:S(2)}, u32[]{:S(2)}) %collective-permute-start.8) | collective-permute-done | bytes 163872 | tf_op jit(solution)/shard_map/ppermute | solution.py:331
  23.8 0.7 %join.1 = (bf16[10,64,128]{2,1,0:T(8,128)(2,1)S(1)}, bf16[12,64,128]{2,1,0:T(8,128)(2,1)S(1)}, bf16[10,64,128]{2,1,0:T(8,128)(2,1)}) custom-call(bf16[10,64,128]{2,1,0:T(8,128)(2,1)S(1)} %merge.1.sent_ref, bf16[10,64,128]{2,1,0:T(8,128)(2,1)S(1)} %collective-permute-done.8.got_ref), custom_call_target="tpu_custom_call" | custom-call | tf_op jit(solution)/shard_map/join/pallas_call | solution.py:411
  24.5 1.9 %collective-permute-start.9 = (bf16[10,64,128]{2,1,0:T(8,128)(2,1)}, bf16[10,64,128]{2,1,0:T(8,128)(2,1)S(1)}, u32[]{:S(2)}, u32[]{:S(2)}) collective-permute-start(bf16[10,64,128]{2,1,0:T(8,128)(2,1)} %get-tuple-element.29), channel_id=1, source_target_pairs={{0,6},{2,4},{4,2},{6,0},{8,14},{10,12},{12,10},{14,8},{1,7},{3,5},... | collective-permute-start | bytes 491528 | tf_op jit(solution)/shard_map/ppermute | solution.py:331
  26.6 1.6 %collective-permute-done.2 = bf16[8,64,128]{2,1,0:T(8,128)(2,1)S(1)} collective-permute-done((bf16[8,64,128]{2,1,0:T(8,128)(2,1)S(1)}, bf16[8,64,128]{2,1,0:T(8,128)(2,1)S(1)}, u32[]{:S(2)}, u32[]{:S(2)}) %collective-permute-start.2) | collective-permute-done | bytes 131104 | tf_op jit(solution)/shard_map/ppermute | solution.py:331
  28.3 1.9 %collective-permute-start.3 = (bf16[8,64,128]{2,1,0:T(8,128)(2,1)S(1)}, bf16[8,64,128]{2,1,0:T(8,128)(2,1)S(1)}, u32[]{:S(2)}, u32[]{:S(2)}) collective-permute-start(bf16[8,64,128]{2,1,0:T(8,128)(2,1)S(1)} %add_convert_fusion.first_ref), channel_id=1, source_target_pairs={{0,8},{2,10},{4,12},{6,14},{8,0},{10,2},{12,4},{14,6},{1,9},{3,11}... | collective-permute-start | bytes 393224 | tf_op jit(solution)/shard_map/ppermute | solution.py:331
  31.2 1.3 %collective-permute-start.14 = (bf16[12,64,128]{2,1,0:T(8,128)(2,1)S(1)}, bf16[12,64,128]{2,1,0:T(8,128)(2,1)S(1)}, u32[]{:S(2)}, u32[]{:S(2)}) collective-permute-start(bf16[12,64,128]{2,1,0:T(8,128)(2,1)S(1)} %get-tuple-element.31), channel_id=1, source_target_pairs={{0,4},{2,6},{4,0},{6,2},{8,12},{10,14},{12,8},{14,10},{1,5},{3,7},... | collective-permute-start | bytes 589832 | tf_op jit(solution)/shard_map/ppermute | solution.py:331
  32.6 4.1 %collective-permute-done.3.second_ref = bf16[8,64,128]{2,1,0:T(8,128)(2,1)S(1)} collective-permute-done((bf16[8,64,128]{2,1,0:T(8,128)(2,1)S(1)}, bf16[8,64,128]{2,1,0:T(8,128)(2,1)S(1)}, u32[]{:S(2)}, u32[]{:S(2)}) %collective-permute-start.3) | collective-permute-done | bytes 131104 | tf_op jit(solution)/shard_map/ppermute | solution.py:331
  36.7 1.3 %collective-permute-start.12 = (bf16[8,64,128]{2,1,0:T(8,128)(2,1)S(1)}, bf16[8,64,128]{2,1,0:T(8,128)(2,1)S(1)}, u32[]{:S(2)}, u32[]{:S(2)}) collective-permute-start(bf16[8,64,128]{2,1,0:T(8,128)(2,1)S(1)} %add.30.refs_6_.refs_0_), channel_id=1, source_target_pairs={{0,6},{2,4},{4,2},{6,0},{8,14},{10,12},{12,10},{14,8},{1,7},{3,5},... | collective-permute-start | bytes 393224 | tf_op jit(solution)/shard_map/ppermute | solution.py:331
  38.0 1.4 %collective-permute-start.11 = (bf16[8,64,128]{2,1,0:T(8,128)(2,1)S(1)}, bf16[8,64,128]{2,1,0:T(8,128)(2,1)S(1)}, u32[]{:S(2)}, u32[]{:S(2)}) collective-permute-start(bf16[8,64,128]{2,1,0:T(8,128)(2,1)S(1)} %add.30.refs_6_.refs_0_), channel_id=1, source_target_pairs={{0,4},{2,6},{4,0},{6,2},{8,12},{10,14},{12,8},{14,10},{1,5},{3,7},... | collective-permute-start | bytes 393224 | tf_op jit(solution)/shard_map/ppermute | solution.py:331
  39.4 0.9 %collective-permute-start.10 = (bf16[8,64,128]{2,1,0:T(8,128)(2,1)S(1)}, bf16[8,64,128]{2,1,0:T(8,128)(2,1)S(1)}, u32[]{:S(2)}, u32[]{:S(2)}) collective-permute-start(bf16[8,64,128]{2,1,0:T(8,128)(2,1)S(1)} %add.30.refs_6_.refs_0_), channel_id=1, source_target_pairs={{0,2},{2,0},{4,6},{6,4},{8,10},{10,8},{12,14},{14,12},{1,3},{3,1},... | collective-permute-start | bytes 393224 | tf_op jit(solution)/shard_map/ppermute | solution.py:331
  40.5 0.9 %small.1.refs_7_ = bf16[2,64,128]{2,1,0:T(8,128)(2,1)S(1)} custom-call(bf16[2,64,128]{2,1,0:T(8,128)(2,1)S(1)} %get-tuple-element.40.refs_0_, bf16[2,64,128]{2,1,0:T(8,128)(2,1)S(1)} %get-tuple-element.38.refs_1_, bf16[2,64,128]{2,1,0:T(8,128)(2,1)S(1)} %slice.58.refs_2_, bf16[2,64,128]{2,1,0:T(8,128)(2,1)S(1)} %get-tuple-element.37.refs_3_, ...), custom_call_target="tpu_custom_call" | custom-call | tf_op jit(solution)/shard_map/small/pallas_call | solution.py:441
  41.6 2.7 %near.1 = (bf16[64,64,128]{2,1,0:T(8,128)(2,1)}, bf16[4,64,128]{2,1,0:T(8,128)(2,1)S(1)}) custom-call(bf16[10,64,128]{2,1,0:T(8,128)(2,1)S(1)} %get-tuple-element.30.refs_0_, bf16[10,64,128]{2,1,0:T(8,128)(2,1)S(1)} %collective-permute-done.13.refs_1_, bf16[12,64,128]{2,1,0:T(8,128)(2,1)S(1)} %collective-permute-done.14.refs_2_, ...), custom_call_target="tpu_custom_call" | custom-call | tf_op jit(solution)/shard_map/near/pallas_call | solution.py:451
  44.9 2.9 %rest.1 = bf16[64,64,128]{2,1,0:T(8,128)(2,1)} custom-call(bf16[8,64,128]{2,1,0:T(8,128)(2,1)S(1)} %add.30.refs_6_.refs_0_, bf16[8,64,128]{2,1,0:T(8,128)(2,1)S(1)} %collective-permute-done.10.refs_1_, bf16[8,64,128]{2,1,0:T(8,128)(2,1)S(1)} %collective-permute-done.11.refs_2_, ...), custom_call_target="tpu_custom_call", output_to_operand_aliasing={{}: (11, {})} | custom-call | tf_op jit(solution)/shard_map/rest/pallas_call | solution.py:460
  (42 shorter events, 3.4 us)
Async XLA Ops:
  0.0 9.0 %copy-start = (bf16[1,64,128,64]{2,3,1,0:T(8,128)(2,1)S(1)}, bf16[1,64,128,64]{2,3,1,0:T(8,128)(2,1)}, u32[]{:S(2)}) copy-start(bf16[1,64,128,64]{2,3,1,0:T(8,128)(2,1)} %param.8) | copy-start | bytes 3145732
  0.0 9.0 %copy-start.2 = (s32[1,64,128]{2,1,0:T(8,128)S(1)}, s32[1,64,128]{2,1,0:T(8,128)}, u32[]{:S(2)}) copy-start(s32[1,64,128]{2,1,0:T(8,128)} %param.9) | copy-start | bytes 98308
  2.3 6.7 %collective-permute-start.4 = (bf16[8,64,128]{2,1,0:T(8,128)(2,1)}, bf16[8,64,128]{2,1,0:T(8,128)(2,1)S(1)}, u32[]{:S(2)}, u32[]{:S(2)}) collective-permute-start(bf16[8,64,128]{2,1,0:T(8,128)(2,1)} %get-tuple-element.26), channel_id=1, source_target_pairs={{0,2},{2,0},{4,6},{6,4},{8,10},{10,8},{12,14},{14,12},{1,3},{3,1},... | collective-permute-start | bytes 393224 | tf_op jit(solution)/shard_map/ppermute | solution.py:331
  5.3 6.6 %collective-permute-start.5 = (bf16[8,64,128]{2,1,0:T(8,128)(2,1)}, bf16[8,64,128]{2,1,0:T(8,128)(2,1)S(1)}, u32[]{:S(2)}, u32[]{:S(2)}) collective-permute-start(bf16[8,64,128]{2,1,0:T(8,128)(2,1)} %get-tuple-element.27), channel_id=1, source_target_pairs={{0,4},{2,6},{4,0},{6,2},{8,12},{10,14},{12,8},{14,10},{1,5},{3,7},... | collective-permute-start | bytes 393224 | tf_op jit(solution)/shard_map/ppermute | solution.py:331
  6.9 6.2 %collective-permute-start.6 = (bf16[8,64,128]{2,1,0:T(8,128)(2,1)}, bf16[8,64,128]{2,1,0:T(8,128)(2,1)S(1)}, u32[]{:S(2)}, u32[]{:S(2)}) collective-permute-start(bf16[8,64,128]{2,1,0:T(8,128)(2,1)} %get-tuple-element.28), channel_id=1, source_target_pairs={{0,6},{2,4},{4,2},{6,0},{8,14},{10,12},{12,10},{14,8},{1,7},{3,5},... | collective-permute-start | bytes 393224 | tf_op jit(solution)/shard_map/ppermute | solution.py:331
  9.0 0.7 %copy-start.5 = (bf16[64,64]{1,0:T(8,128)(2,1)S(1)}, bf16[64,64]{1,0:T(8,128)(2,1)}, u32[]{:S(2)}) copy-start(bf16[64,64]{1,0:T(8,128)(2,1)} %column_ref.1) | copy-start | bytes 24580
  9.7 0.7 %copy-start.6 = (bf16[128,64]{0,1:T(8,128)(2,1)S(1)}, bf16[128,64]{0,1:T(8,128)(2,1)}, u32[]{:S(2)}) copy-start(bf16[128,64]{0,1:T(8,128)(2,1)} %param.12) | copy-start | bytes 49156
  10.4 2.6 %copy-start.3 = (f32[8,64,128]{2,1,0:T(8,128)S(1)}, f32[8,64,128]{2,1,0:T(8,128)}, u32[]{:S(2)}) copy-start(f32[8,64,128]{2,1,0:T(8,128)} %get-tuple-element.25.own_ref) | copy-start | bytes 786436
  11.3 1.7 %collective-permute-start.7 = (f32[64,256]{1,0:T(8,128)S(1)}, f32[64,256]{1,0:T(8,128)S(1)}, u32[]{:S(2)}, u32[]{:S(2)}) collective-permute-start(f32[64,256]{1,0:T(8,128)S(1)} %sums.1.message_ref), channel_id=1, source_target_pairs={{0,1},{1,0},{2,3},{3,2},{4,5},{5,4},{6,7},{7,6},{8,9},{9,8},{10,11... | collective-permute-start | bytes 196616 | tf_op jit(solution)/shard_map/ppermute | solution.py:331
  13.1 2.9 %copy-start.8 = (bf16[1,64]{1,0:T(2,128)(2,1)S(1)}, bf16[1,64]{1,0:T(2,128)(2,1)}, u32[]{:S(2)}) copy-start(bf16[1,64]{1,0:T(2,128)(2,1)} %row_hbm.1) | copy-start | bytes 388
  13.1 10.6 %collective-permute-start.8 = (bf16[10,64,128]{2,1,0:T(8,128)(2,1)S(1)}, bf16[10,64,128]{2,1,0:T(8,128)(2,1)S(1)}, u32[]{:S(2)}, u32[]{:S(2)}) collective-permute-start(bf16[10,64,128]{2,1,0:T(8,128)(2,1)S(1)} %merge.1.sent_ref), channel_id=1, source_target_pairs={{0,8},{2,10},{4,12},{6,14},{8,0},{10,2},{12,4},{14,6},{1,9},{3,11}... | collective-permute-start | bytes 491528 | tf_op jit(solution)/shard_map/ppermute | solution.py:331
  16.1 14.1 %copy-start.1 = (bf16[3,2,3,3,64,64]{5,4,3,2,1,0:T(8,128)(2,1)S(1)}, bf16[3,2,3,3,64,64]{5,4,3,2,1,0:T(8,128)(2,1)}, u32[]{:S(2)}) copy-start(bf16[3,2,3,3,64,64]{5,4,3,2,1,0:T(8,128)(2,1)} %kernel_ref.1) | copy-start | bytes 1327108
  16.2 10.5 %collective-permute-start = (bf16[8,64,128]{2,1,0:T(8,128)(2,1)S(1)}, bf16[8,64,128]{2,1,0:T(8,128)(2,1)S(1)}, u32[]{:S(2)}, u32[]{:S(2)}) collective-permute-start(bf16[8,64,128]{2,1,0:T(8,128)(2,1)S(1)} %get-tuple-element.22), channel_id=1, source_target_pairs={{0,2},{2,0},{4,6},{6,4},{8,10},{10,8},{12,14},{14,12},{1,3},{3,1},... | collective-permute-start | bytes 393224 | tf_op jit(solution)/shard_map/ppermute | solution.py:331
  17.7 8.9 %collective-permute-start.1 = (bf16[8,64,128]{2,1,0:T(8,128)(2,1)S(1)}, bf16[8,64,128]{2,1,0:T(8,128)(2,1)S(1)}, u32[]{:S(2)}, u32[]{:S(2)}) collective-permute-start(bf16[8,64,128]{2,1,0:T(8,128)(2,1)S(1)} %get-tuple-element.23), channel_id=1, source_target_pairs={{0,4},{2,6},{4,0},{6,2},{8,12},{10,14},{12,8},{14,10},{1,5},{3,7},... | collective-permute-start | bytes 393224 | tf_op jit(solution)/shard_map/ppermute | solution.py:331
  19.3 8.9 %collective-permute-start.2 = (bf16[8,64,128]{2,1,0:T(8,128)(2,1)S(1)}, bf16[8,64,128]{2,1,0:T(8,128)(2,1)S(1)}, u32[]{:S(2)}, u32[]{:S(2)}) collective-permute-start(bf16[8,64,128]{2,1,0:T(8,128)(2,1)S(1)} %get-tuple-element.24), channel_id=1, source_target_pairs={{0,6},{2,4},{4,2},{6,0},{8,14},{10,12},{12,10},{14,8},{1,7},{3,5},... | collective-permute-start | bytes 393224 | tf_op jit(solution)/shard_map/ppermute | solution.py:331
  24.5 12.2 %collective-permute-start.9 = (bf16[10,64,128]{2,1,0:T(8,128)(2,1)}, bf16[10,64,128]{2,1,0:T(8,128)(2,1)S(1)}, u32[]{:S(2)}, u32[]{:S(2)}) collective-permute-start(bf16[10,64,128]{2,1,0:T(8,128)(2,1)} %get-tuple-element.29), channel_id=1, source_target_pairs={{0,6},{2,4},{4,2},{6,0},{8,14},{10,12},{12,10},{14,8},{1,7},{3,5},... | collective-permute-start | bytes 491528 | tf_op jit(solution)/shard_map/ppermute | solution.py:331
  26.4 13.9 %collective-permute-start.13 = (bf16[10,64,128]{2,1,0:T(8,128)(2,1)S(1)}, bf16[10,64,128]{2,1,0:T(8,128)(2,1)S(1)}, u32[]{:S(2)}, u32[]{:S(2)}) collective-permute-start(bf16[10,64,128]{2,1,0:T(8,128)(2,1)S(1)} %get-tuple-element.30.refs_0_), channel_id=1, source_target_pairs={{0,2},{2,0},{4,6},{6,4},{8,10},{10,8},{12,14},{14,12},{1,3},{3,1},... | collective-permute-start | bytes 491528 | tf_op jit(solution)/shard_map/ppermute | solution.py:331
  28.3 8.4 %collective-permute-start.3 = (bf16[8,64,128]{2,1,0:T(8,128)(2,1)S(1)}, bf16[8,64,128]{2,1,0:T(8,128)(2,1)S(1)}, u32[]{:S(2)}, u32[]{:S(2)}) collective-permute-start(bf16[8,64,128]{2,1,0:T(8,128)(2,1)S(1)} %add_convert_fusion.first_ref), channel_id=1, source_target_pairs={{0,8},{2,10},{4,12},{6,14},{8,0},{10,2},{12,4},{14,6},{1,9},{3,11}... | collective-permute-start | bytes 393224 | tf_op jit(solution)/shard_map/ppermute | solution.py:331
  31.2 9.1 %collective-permute-start.14 = (bf16[12,64,128]{2,1,0:T(8,128)(2,1)S(1)}, bf16[12,64,128]{2,1,0:T(8,128)(2,1)S(1)}, u32[]{:S(2)}, u32[]{:S(2)}) collective-permute-start(bf16[12,64,128]{2,1,0:T(8,128)(2,1)S(1)} %get-tuple-element.31), channel_id=1, source_target_pairs={{0,4},{2,6},{4,0},{6,2},{8,12},{10,14},{12,8},{14,10},{1,5},{3,7},... | collective-permute-start | bytes 589832 | tf_op jit(solution)/shard_map/ppermute | solution.py:331
  36.7 7.6 %collective-permute-start.12 = (bf16[8,64,128]{2,1,0:T(8,128)(2,1)S(1)}, bf16[8,64,128]{2,1,0:T(8,128)(2,1)S(1)}, u32[]{:S(2)}, u32[]{:S(2)}) collective-permute-start(bf16[8,64,128]{2,1,0:T(8,128)(2,1)S(1)} %add.30.refs_6_.refs_0_), channel_id=1, source_target_pairs={{0,6},{2,4},{4,2},{6,0},{8,14},{10,12},{12,10},{14,8},{1,7},{3,5},... | collective-permute-start | bytes 393224 | tf_op jit(solution)/shard_map/ppermute | solution.py:331
  38.0 6.4 %collective-permute-start.11 = (bf16[8,64,128]{2,1,0:T(8,128)(2,1)S(1)}, bf16[8,64,128]{2,1,0:T(8,128)(2,1)S(1)}, u32[]{:S(2)}, u32[]{:S(2)}) collective-permute-start(bf16[8,64,128]{2,1,0:T(8,128)(2,1)S(1)} %add.30.refs_6_.refs_0_), channel_id=1, source_target_pairs={{0,4},{2,6},{4,0},{6,2},{8,12},{10,14},{12,8},{14,10},{1,5},{3,7},... | collective-permute-start | bytes 393224 | tf_op jit(solution)/shard_map/ppermute | solution.py:331
  39.4 5.5 %collective-permute-start.10 = (bf16[8,64,128]{2,1,0:T(8,128)(2,1)S(1)}, bf16[8,64,128]{2,1,0:T(8,128)(2,1)S(1)}, u32[]{:S(2)}, u32[]{:S(2)}) collective-permute-start(bf16[8,64,128]{2,1,0:T(8,128)(2,1)S(1)} %add.30.refs_6_.refs_0_), channel_id=1, source_target_pairs={{0,2},{2,0},{4,6},{6,4},{8,10},{10,8},{12,14},{14,12},{1,3},{3,1},... | collective-permute-start | bytes 393224 | tf_op jit(solution)/shard_map/ppermute | solution.py:331
  40.4 1.3 %collective-permute-start.15 = (bf16[2,64,128]{2,1,0:T(8,128)(2,1)S(1)}, bf16[2,64,128]{2,1,0:T(8,128)(2,1)S(1)}, u32[]{:S(2)}, u32[]{:S(2)}) collective-permute-start(bf16[2,64,128]{2,1,0:T(8,128)(2,1)S(1)} %slice_select_fusion.1), channel_id=1, source_target_pairs={{0,1},{1,0},{2,3},{3,2},{4,5},{5,4},{6,7},{7,6},{8,9},{9,8},{10,11... | collective-permute-start | bytes 98312 | tf_op jit(solution)/shard_map/ppermute | solution.py:331
  40.5 1.2 %copy-start.4 = (bf16[128,64]{0,1:T(8,128)(2,1)S(1)}, bf16[128,64]{0,1:T(8,128)(2,1)}, u32[]{:S(2)}) copy-start(bf16[128,64]{0,1:T(8,128)(2,1)} %param.15) | copy-start | bytes 49156
  (1 other events, 0.7 us)

commit v3 on v2

--- a/solution.py
+++ b/solution.py
@@ -140,8 +140,8 @@
     return pl.multiple_of(chunk_base(chunk, core, rows) + jnp.bitwise_xor(low, d) * quarter, quarter)
 
 
-def fetch_kernel(row_hbm, vox_hbm, occ_hbm, *refs):
-    out_refs, (row_ref, vox_ref, occ_ref, row_sem, vox_sem, occ_sem) = refs[:4], refs[4:]
+def fetch_kernel(row_hbm, vox_hbm, occ_hbm, column_hbm, depth_hbm, *refs):
+    out_refs, more_refs, (row_ref, vox_ref, occ_ref, row_sem, vox_sem, occ_sem, more_sem) = refs[:4], refs[4:6], refs[6:]
     rows = vox_hbm.shape[0]
     quarter = rows // 8
     copies = [pltpu.make_async_copy(row_hbm, row_ref, row_sem)]
@@ -149,6 +149,8 @@
         part = pl.ds(quarter_at(rows, 0, d), quarter)
         copies.append(pltpu.make_async_copy(vox_hbm.at[part], vox_ref.at[d], vox_sem.at[d]))
         copies.append(pltpu.make_async_copy(occ_hbm.at[part], occ_ref.at[d], occ_sem.at[d]))
+    for i, source in enumerate((column_hbm, depth_hbm)):
+        copies.append(pltpu.make_async_copy(source, more_refs[i], more_sem.at[i]))
     for copy in copies:
         copy.start()
     for copy in copies:
@@ -157,7 +159,8 @@
         weighted(vox_ref[d], occ_ref[d], row_ref, out_refs[d])
 
 
-def front_kernel(row_ref, vox_ref, occ_ref, *out_refs):
+def front_kernel(row_ref, vox_ref, occ_ref, after_ref, *out_refs):
+    del after_ref
     rows = vox_ref.shape[0]
     for d in (1, 2, 3, 0):
         part = pl.ds(quarter_at(rows, 1, d), rows // 8)
@@ -194,7 +197,8 @@
     out_ref[:, z:] = xy.astype(bf16).astype(f32)
 
 
-def merge_kernel(own_ref, first_ref, second_ref, third_ref, message_ref, other_ref, out_ref):
+def merge_kernel(own_ref, first_ref, second_ref, third_ref, message_ref, other_ref, after_ref, out_ref):
+    del after_ref
     quarter, c, z = own_ref.shape
     for i in range(quarter):
         total = own_ref[i] + first_ref[i].astype(f32) + second_ref[i].astype(f32) + third_ref[i].astype(f32)
@@ -211,7 +215,8 @@
     out_ref[...] = (first_ref[...].astype(f32) + second_ref[...].astype(f32)).astype(bf16)
 
 
-def join_kernel(sent_ref, got_ref, first_ref, second_ref, third_ref):
+def join_kernel(sent_ref, got_ref, after_ref, first_ref, second_ref, third_ref):
+    del after_ref
     quarter = sent_ref.shape[0] - 2
     for i in range(quarter):
         total = (sent_ref[i].astype(f32) + got_ref[i].astype(f32)).astype(bf16)
@@ -376,17 +381,16 @@
         pltpu.SemaphoreType.DMA,
         pltpu.SemaphoreType.DMA((4,)),
         pltpu.SemaphoreType.DMA((4,)),
+        pltpu.SemaphoreType.DMA((2,)),
     ]
     hbm = pl.BlockSpec(memory_space=pltpu.HBM)
-    inputs = row_weights, vox, occ
-    fronts = call(fetch_kernel, "fetch", shapes, [hbm] * 3, scratch, mib=62)(*inputs)
-    fronts += call(front_kernel, "front", shapes, [vmem()] * 3)(*inputs)
-    owns = [fronts[0], fronts[4]]
-    gots = [[swap(fronts[4 * chunk + d], "gx", d) for d in (1, 2, 3)] for chunk in range(2)]
-
-    message = call(
-        sums_kernel, "sums", jax.ShapeDtypeStruct((c, 2 * z), f32), [vmem()] * 4 + [anywhere()]
-    )(vox, occ, column_weights, depth_weights.T, gots[0][0])
+    more = column_weights, depth_weights.T
+    more_shapes = [jax.ShapeDtypeStruct(value.shape, bf16) for value in more]
+    *first, column, depth = call(fetch_kernel, "fetch", shapes + more_shapes, [hbm] * 5, scratch, mib=62)(
+        row_weights, vox, occ, *more
+    )
+    partners = lambda values: [swap(value, "gx", d) for d, value in zip((1, 2, 3), values)]
+    first_got = partners(first[1:])
     stacked = plane_kernels.shape[1:2] + (3 * c, 3 * c)
     small_weights, main_weights, expanded = call(
         weights_kernel,
@@ -397,9 +401,15 @@
             jax.ShapeDtypeStruct(expand_weight.shape[::-1], bf16),
         ],
         [vmem()] * 2 + [anywhere()],
-    )(plane_kernels, expand_weight, gots[1][0])
-    merged = call(merge_kernel, "merge", piece(bf16, quarter + 2), [vmem()] * 6)(
-        owns[0], *gots[0], message, swap(message, "gy", 1)
+    )(plane_kernels, expand_weight, first_got[0])
+    message = call(
+        sums_kernel, "sums", jax.ShapeDtypeStruct((c, 2 * z), f32), [vmem()] * 4 + [anywhere()]
+    )(vox, occ, column, depth, expanded)
+    own, *send = call(front_kernel, "front", shapes, [vmem()] * 3 + [anywhere()])(row_weights, vox, occ, message)
+    owns, gots = [first[0], own], [first_got, partners(send)]
+
+    merged = call(merge_kernel, "merge", piece(bf16, quarter + 2), [vmem()] * 6 + [anywhere()])(
+        owns[0], *gots[0], message, swap(message, "gy", 1), owns[1]
     )
     second = owns[1]
     for got in gots[1]:
@@ -409,8 +419,8 @@
     planes = merged[quarter:]
     if gx_size == 8:
         sent = call(
-            join_kernel, "join", [piece(bf16, quarter + n) for n in (2, 4, 2)], [vmem()] * 2
-        )(merged, swap(merged, "gx", 4))
+            join_kernel, "join", [piece(bf16, quarter + n) for n in (2, 4, 2)], [vmem()] * 2 + [anywhere()]
+        )(merged, swap(merged, "gx", 4), gots[1][2])
         got = [swap(value, "gx", d) for d, value in zip((1, 2, 3), sent)]
         second = call(add_kernel, "add", piece(bf16), [vmem()] * 2 + [anywhere()])(second, swap(second, "gx", 4), got[2])
         pieces = [[sent[0]] + got, None]

time: 48.3 us -> 47.8 us (0.990)
  starting transfers between devices: 20 us -> 21.2 us
  local copies, waits for them, and re-layouts: 2.18 us -> 1.41 us
  Pallas kernels: 11 us -> 10.4 us
    ppermute x16, starting transfers between devices: 20 us -> 21.2 us  [swap(): lax.ppermute(value, axis, [(i, i ^ bit) for i in range(lax.axis_size(axis...]
    unnamed x18 -> x22, local copies, waits for them, and re-layouts: 2.18 us -> 1.4 us
    pallas_call x1, Pallas kernels: 0.72 us -> 0.05 us  [shards(): call(join_kernel, 'join', [piece(bf16, quarter + n) for n in (2, 4, 2)],...]
  transfers between devices with their start and end apart: 16 -> 16, of which waited for: 8 -> 8; matrix products, arithmetic and copies ran while one was open for 0% -> 0% of each run, Pallas kernels for 12% -> 11%
where the time goes in v3:
time: 47.8 us; the launch traced here: 47.3 us
  starting transfers between devices  21.2 us (44%)
  waiting for transfers between devices  13.9 us (29%)
  Pallas kernels  10.4 us (22%)
  local copies, waits for them, and re-layouts  1.41 us (3%)
    ppermute x16, starting transfers between devices, swap(): lax.ppermute(value, axis, [(i, i ^ bit) for i in range(lax.axis_size(axis...  21.2 us
    ppermute x16, waiting for transfers between devices, swap(): lax.ppermute(value, axis, [(i, i ^ bit) for i in range(lax.axis_size(axis...  13.9 us
    pallas_call x1, Pallas kernels, shards(): pl.pallas_call(rest_kernel, out_shape=whole, in_specs=[vmem()] * 11 + [hb...  2.94 us
    pallas_call x1, Pallas kernels, shards(): pl.pallas_call(near_kernel, out_shape=[whole, piece(bf16, 4)], in_specs=[...  2.72 us
    pallas_call x1, Pallas kernels, shards(): call(fetch_kernel, 'fetch', shapes + more_shapes, [hbm] * 5, scratch, mib...  2.32 us
    unnamed x22, local copies, waits for them, and re-layouts  1.4 us
  transfers between devices with their start and end apart: 16, of which 8 were waited for; matrix products, arithmetic and copies ran while one was open for 0% of the time, Pallas kernels for 11%

profile of v3, /device:TPU:0, one launch (start us, length us, event | category | flops | bytes accessed | tf_op | source)
XLA Modules:
  0.0 47.3 jit_solution(17081131614770508737)
XLA Ops:
  0.0 2.3 %fetch.1 = (f32[8,64,128]{2,1,0:T(8,128)}, bf16[8,64,128]{2,1,0:T(8,128)(2,1)}, bf16[8,64,128]{2,1,0:T(8,128)(2,1)}, bf16[8,64,128]{2,1,0:T(8,128)(2,1)}, bf16[6...) custom-call(bf16[1,64]{1,0:T(2,128)(2,1)} %row_ref.1, bf16[64,64,128]{2,1,0:T(8,128)(2,1)} %bitcast.9, s32[64,128]{1,0:T(8,128)} %bitcast.14, ...), custom_call_target="tpu_custom_call" | custom-call | tf_op jit(solution)/shard_map/fetch/pallas_call | solution.py:389
  2.3 3.0 %collective-permute-start = (bf16[8,64,128]{2,1,0:T(8,128)(2,1)}, bf16[8,64,128]{2,1,0:T(8,128)(2,1)S(1)}, u32[]{:S(2)}, u32[]{:S(2)}) collective-permute-start(bf16[8,64,128]{2,1,0:T(8,128)(2,1)} %get-tuple-element.25), channel_id=1, source_target_pairs={{0,2},{2,0},{4,6},{6,4},{8,10},{10,8},{12,14},{14,12},{1,3},{3,1},... | collective-permute-start | bytes 393224 | tf_op jit(solution)/shard_map/ppermute | solution.py:336
  5.3 1.6 %collective-permute-start.5 = (bf16[8,64,128]{2,1,0:T(8,128)(2,1)}, bf16[8,64,128]{2,1,0:T(8,128)(2,1)S(1)}, u32[]{:S(2)}, u32[]{:S(2)}) collective-permute-start(bf16[8,64,128]{2,1,0:T(8,128)(2,1)} %get-tuple-element.32), channel_id=1, source_target_pairs={{0,4},{2,6},{4,0},{6,2},{8,12},{10,14},{12,8},{14,10},{1,5},{3,7},... | collective-permute-start | bytes 393224 | tf_op jit(solution)/shard_map/ppermute | solution.py:336
  6.9 2.1 %collective-permute-done.after_ref.first_ref = bf16[8,64,128]{2,1,0:T(8,128)(2,1)S(1)} collective-permute-done((bf16[8,64,128]{2,1,0:T(8,128)(2,1)}, bf16[8,64,128]{2,1,0:T(8,128)(2,1)S(1)}, u32[]{:S(2)}, u32[]{:S(2)}) %collective-permute-start) | collective-permute-done | bytes 131104 | tf_op jit(solution)/shard_map/ppermute | solution.py:336
  9.1 0.7 %copy-done.7 = bf16[64,128]{1,0:T(8,128)(2,1)S(1)} copy-done((bf16[64,128]{1,0:T(8,128)(2,1)S(1)}, bf16[64,128]{1,0:T(8,128)(2,1)}, u32[]{:S(2)}) %copy-start.7) | copy-done | bytes 16408
  10.5 0.9 %sums.1.after_ref.message_ref = f32[64,256]{1,0:T(8,128)S(1)} custom-call(bf16[64,64,128]{2,1,0:T(8,128)(2,1)S(1)} %bitcast.10, s32[64,128]{1,0:T(8,128)S(1)} %bitcast.15, bf16[64,64]{1,0:T(8,128)(2,1)S(1)} %copy-done.8, bf16[64,128]{1,0:T(8,128)(2,1)S(1)} %copy-done.9, bf16[128,64]{1,0:T(8,128)(2,1)S(1)} %get-tuple-element.26.after_ref.refs_9_), custom_call_target="tpu_custom_call" | custom-call | tf_op jit(solution)/shard_map/sums/pallas_call | solution.py:405
  11.9 1.2 %collective-permute-done.6.third_ref = bf16[8,64,128]{2,1,0:T(8,128)(2,1)S(1)} collective-permute-done((bf16[8,64,128]{2,1,0:T(8,128)(2,1)}, bf16[8,64,128]{2,1,0:T(8,128)(2,1)S(1)}, u32[]{:S(2)}, u32[]{:S(2)}) %collective-permute-start.6) | collective-permute-done | bytes 131104 | tf_op jit(solution)/shard_map/ppermute | solution.py:336
  13.2 2.8 %collective-permute-start.8 = (bf16[10,64,128]{2,1,0:T(8,128)(2,1)S(1)}, bf16[10,64,128]{2,1,0:T(8,128)(2,1)S(1)}, u32[]{:S(2)}, u32[]{:S(2)}) collective-permute-start(bf16[10,64,128]{2,1,0:T(8,128)(2,1)S(1)} %merge.1.sent_ref), channel_id=1, source_target_pairs={{0,8},{2,10},{4,12},{6,14},{8,0},{10,2},{12,4},{14,6},{1,9},{3,11}... | collective-permute-start | bytes 491528 | tf_op jit(solution)/shard_map/ppermute | solution.py:336
  16.0 2.5 %collective-permute-start.3 = (bf16[8,64,128]{2,1,0:T(8,128)(2,1)S(1)}, bf16[8,64,128]{2,1,0:T(8,128)(2,1)S(1)}, u32[]{:S(2)}, u32[]{:S(2)}) collective-permute-start(bf16[8,64,128]{2,1,0:T(8,128)(2,1)S(1)} %get-tuple-element.30), channel_id=1, source_target_pairs={{0,6},{2,4},{4,2},{6,0},{8,14},{10,12},{12,10},{14,8},{1,7},{3,5},... | collective-permute-start | bytes 393224 | tf_op jit(solution)/shard_map/ppermute | solution.py:336
  18.5 0.5 %collective-permute-start.1 = (bf16[8,64,128]{2,1,0:T(8,128)(2,1)S(1)}, bf16[8,64,128]{2,1,0:T(8,128)(2,1)S(1)}, u32[]{:S(2)}, u32[]{:S(2)}) collective-permute-start(bf16[8,64,128]{2,1,0:T(8,128)(2,1)S(1)} %get-tuple-element.28), channel_id=1, source_target_pairs={{0,2},{2,0},{4,6},{6,4},{8,10},{10,8},{12,14},{14,12},{1,3},{3,1},... | collective-permute-start | bytes 393224 | tf_op jit(solution)/shard_map/ppermute | solution.py:336
  19.5 3.8 %collective-permute-done.3.after_ref = bf16[8,64,128]{2,1,0:T(8,128)(2,1)S(1)} collective-permute-done((bf16[8,64,128]{2,1,0:T(8,128)(2,1)S(1)}, bf16[8,64,128]{2,1,0:T(8,128)(2,1)S(1)}, u32[]{:S(2)}, u32[]{:S(2)}) %collective-permute-start.3) | collective-permute-done | bytes 131104 | tf_op jit(solution)/shard_map/ppermute | solution.py:336
  23.9 2.9 %collective-permute-start.9 = (bf16[10,64,128]{2,1,0:T(8,128)(2,1)S(1)}, bf16[10,64,128]{2,1,0:T(8,128)(2,1)S(1)}, u32[]{:S(2)}, u32[]{:S(2)}) collective-permute-start(bf16[10,64,128]{2,1,0:T(8,128)(2,1)S(1)} %get-tuple-element.34), channel_id=1, source_target_pairs={{0,6},{2,4},{4,2},{6,0},{8,14},{10,12},{12,10},{14,8},{1,7},{3,5},... | collective-permute-start | bytes 491528 | tf_op jit(solution)/shard_map/ppermute | solution.py:336
  26.8 1.6 %collective-permute-start.13 = (bf16[10,64,128]{2,1,0:T(8,128)(2,1)S(1)}, bf16[10,64,128]{2,1,0:T(8,128)(2,1)S(1)}, u32[]{:S(2)}, u32[]{:S(2)}) collective-permute-start(bf16[10,64,128]{2,1,0:T(8,128)(2,1)S(1)} %get-tuple-element.35.refs_0_), channel_id=1, source_target_pairs={{0,2},{2,0},{4,6},{6,4},{8,10},{10,8},{12,14},{14,12},{1,3},{3,1},... | collective-permute-start | bytes 491528 | tf_op jit(solution)/shard_map/ppermute | solution.py:336
  28.6 1.3 %collective-permute-start.4 = (bf16[8,64,128]{2,1,0:T(8,128)(2,1)S(1)}, bf16[8,64,128]{2,1,0:T(8,128)(2,1)S(1)}, u32[]{:S(2)}, u32[]{:S(2)}) collective-permute-start(bf16[8,64,128]{2,1,0:T(8,128)(2,1)S(1)} %add_convert_fusion.first_ref), channel_id=1, source_target_pairs={{0,8},{2,10},{4,12},{6,14},{8,0},{10,2},{12,4},{14,6},{1,9},{3,11}... | collective-permute-start | bytes 393224 | tf_op jit(solution)/shard_map/ppermute | solution.py:336
  29.8 0.8 %collective-permute-start.14 = (bf16[12,64,128]{2,1,0:T(8,128)(2,1)S(1)}, bf16[12,64,128]{2,1,0:T(8,128)(2,1)S(1)}, u32[]{:S(2)}, u32[]{:S(2)}) collective-permute-start(bf16[12,64,128]{2,1,0:T(8,128)(2,1)S(1)} %get-tuple-element.36), channel_id=1, source_target_pairs={{0,4},{2,6},{4,0},{6,2},{8,12},{10,14},{12,8},{14,10},{1,5},{3,7},... | collective-permute-start | bytes 589832 | tf_op jit(solution)/shard_map/ppermute | solution.py:336
  30.6 4.9 %collective-permute-done.4.second_ref = bf16[8,64,128]{2,1,0:T(8,128)(2,1)S(1)} collective-permute-done((bf16[8,64,128]{2,1,0:T(8,128)(2,1)S(1)}, bf16[8,64,128]{2,1,0:T(8,128)(2,1)S(1)}, u32[]{:S(2)}, u32[]{:S(2)}) %collective-permute-start.4) | collective-permute-done | bytes 131104 | tf_op jit(solution)/shard_map/ppermute | solution.py:336
  35.6 2.2 %collective-permute-start.12 = (bf16[8,64,128]{2,1,0:T(8,128)(2,1)S(1)}, bf16[8,64,128]{2,1,0:T(8,128)(2,1)S(1)}, u32[]{:S(2)}, u32[]{:S(2)}) collective-permute-start(bf16[8,64,128]{2,1,0:T(8,128)(2,1)S(1)} %add.30.refs_6_.refs_0_), channel_id=1, source_target_pairs={{0,6},{2,4},{4,2},{6,0},{8,14},{10,12},{12,10},{14,8},{1,7},{3,5},... | collective-permute-start | bytes 393224 | tf_op jit(solution)/shard_map/ppermute | solution.py:336
  37.8 0.8 %collective-permute-start.11 = (bf16[8,64,128]{2,1,0:T(8,128)(2,1)S(1)}, bf16[8,64,128]{2,1,0:T(8,128)(2,1)S(1)}, u32[]{:S(2)}, u32[]{:S(2)}) collective-permute-start(bf16[8,64,128]{2,1,0:T(8,128)(2,1)S(1)} %add.30.refs_6_.refs_0_), channel_id=1, source_target_pairs={{0,4},{2,6},{4,0},{6,2},{8,12},{10,14},{12,8},{14,10},{1,5},{3,7},... | collective-permute-start | bytes 393224 | tf_op jit(solution)/shard_map/ppermute | solution.py:336
  38.6 0.5 %collective-permute-start.10 = (bf16[8,64,128]{2,1,0:T(8,128)(2,1)S(1)}, bf16[8,64,128]{2,1,0:T(8,128)(2,1)S(1)}, u32[]{:S(2)}, u32[]{:S(2)}) collective-permute-start(bf16[8,64,128]{2,1,0:T(8,128)(2,1)S(1)} %add.30.refs_6_.refs_0_), channel_id=1, source_target_pairs={{0,2},{2,0},{4,6},{6,4},{8,10},{10,8},{12,14},{14,12},{1,3},{3,1},... | collective-permute-start | bytes 393224 | tf_op jit(solution)/shard_map/ppermute | solution.py:336
  39.2 0.6 %collective-permute-done.14.refs_2_ = bf16[12,64,128]{2,1,0:T(8,128)(2,1)S(1)} collective-permute-done((bf16[12,64,128]{2,1,0:T(8,128)(2,1)S(1)}, bf16[12,64,128]{2,1,0:T(8,128)(2,1)S(1)}, u32[]{:S(2)}, u32[]{:S(2)}) %collective-permute-start.14) | collective-permute-done | bytes 196640 | tf_op jit(solution)/shard_map/ppermute | solution.py:336
  40.1 0.9 %small.1.refs_7_ = bf16[2,64,128]{2,1,0:T(8,128)(2,1)S(1)} custom-call(bf16[2,64,128]{2,1,0:T(8,128)(2,1)S(1)} %get-tuple-element.44.refs_0_, bf16[2,64,128]{2,1,0:T(8,128)(2,1)S(1)} %get-tuple-element.42.refs_1_, bf16[2,64,128]{2,1,0:T(8,128)(2,1)S(1)} %slice.58.refs_2_, bf16[2,64,128]{2,1,0:T(8,128)(2,1)S(1)} %get-tuple-element.41.refs_3_, ...), custom_call_target="tpu_custom_call" | custom-call | tf_op jit(solution)/shard_map/small/pallas_call | solution.py:451
  41.1 2.7 %near.1 = (bf16[64,64,128]{2,1,0:T(8,128)(2,1)}, bf16[4,64,128]{2,1,0:T(8,128)(2,1)S(1)}) custom-call(bf16[10,64,128]{2,1,0:T(8,128)(2,1)S(1)} %get-tuple-element.35.refs_0_, bf16[10,64,128]{2,1,0:T(8,128)(2,1)S(1)} %collective-permute-done.13.refs_1_, bf16[12,64,128]{2,1,0:T(8,128)(2,1)S(1)} %collective-permute-done.14.refs_2_, ...), custom_call_target="tpu_custom_call" | custom-call | tf_op jit(solution)/shard_map/near/pallas_call | solution.py:461
  43.8 0.5 %collective-permute-done.11.refs_2_ = bf16[8,64,128]{2,1,0:T(8,128)(2,1)S(1)} collective-permute-done((bf16[8,64,128]{2,1,0:T(8,128)(2,1)S(1)}, bf16[8,64,128]{2,1,0:T(8,128)(2,1)S(1)}, u32[]{:S(2)}, u32[]{:S(2)}) %collective-permute-start.11) | collective-permute-done | bytes 131104 | tf_op jit(solution)/shard_map/ppermute | solution.py:336
  44.4 2.9 %rest.1 = bf16[64,64,128]{2,1,0:T(8,128)(2,1)} custom-call(bf16[8,64,128]{2,1,0:T(8,128)(2,1)S(1)} %add.30.refs_6_.refs_0_, bf16[8,64,128]{2,1,0:T(8,128)(2,1)S(1)} %collective-permute-done.10.refs_1_, bf16[8,64,128]{2,1,0:T(8,128)(2,1)S(1)} %collective-permute-done.11.refs_2_, ...), custom_call_target="tpu_custom_call", output_to_operand_aliasing={{}: (11, {})} | custom-call | tf_op jit(solution)/shard_map/rest/pallas_call | solution.py:470
  (46 shorter events, 2.8 us)
Async XLA Ops:
  0.0 9.1 %copy-start.1 = (bf16[3,2,3,3,64,64]{5,4,3,2,1,0:T(8,128)(2,1)S(1)}, bf16[3,2,3,3,64,64]{5,4,3,2,1,0:T(8,128)(2,1)}, u32[]{:S(2)}) copy-start(bf16[3,2,3,3,64,64]{5,4,3,2,1,0:T(8,128)(2,1)} %kernel_ref.1) | copy-start | bytes 1327108
  0.0 10.1 %copy-start = (bf16[1,64,128,64]{2,3,1,0:T(8,128)(2,1)S(1)}, bf16[1,64,128,64]{2,3,1,0:T(8,128)(2,1)}, u32[]{:S(2)}) copy-start(bf16[1,64,128,64]{2,3,1,0:T(8,128)(2,1)} %param.8) | copy-start | bytes 3145732
  2.3 6.7 %collective-permute-start = (bf16[8,64,128]{2,1,0:T(8,128)(2,1)}, bf16[8,64,128]{2,1,0:T(8,128)(2,1)S(1)}, u32[]{:S(2)}, u32[]{:S(2)}) collective-permute-start(bf16[8,64,128]{2,1,0:T(8,128)(2,1)} %get-tuple-element.25), channel_id=1, source_target_pairs={{0,2},{2,0},{4,6},{6,4},{8,10},{10,8},{12,14},{14,12},{1,3},{3,1},... | collective-permute-start | bytes 393224 | tf_op jit(solution)/shard_map/ppermute | solution.py:336
  5.3 6.6 %collective-permute-start.5 = (bf16[8,64,128]{2,1,0:T(8,128)(2,1)}, bf16[8,64,128]{2,1,0:T(8,128)(2,1)S(1)}, u32[]{:S(2)}, u32[]{:S(2)}) collective-permute-start(bf16[8,64,128]{2,1,0:T(8,128)(2,1)} %get-tuple-element.32), channel_id=1, source_target_pairs={{0,4},{2,6},{4,0},{6,2},{8,12},{10,14},{12,8},{14,10},{1,5},{3,7},... | collective-permute-start | bytes 393224 | tf_op jit(solution)/shard_map/ppermute | solution.py:336
  6.9 3.2 %copy-start.2 = (s32[1,64,128]{2,1,0:T(8,128)S(1)}, s32[1,64,128]{2,1,0:T(8,128)}, u32[]{:S(2)}) copy-start(s32[1,64,128]{2,1,0:T(8,128)} %param.9) | copy-start | bytes 98308
  6.9 6.2 %collective-permute-start.6 = (bf16[8,64,128]{2,1,0:T(8,128)(2,1)}, bf16[8,64,128]{2,1,0:T(8,128)(2,1)S(1)}, u32[]{:S(2)}, u32[]{:S(2)}) collective-permute-start(bf16[8,64,128]{2,1,0:T(8,128)(2,1)} %get-tuple-element.33), channel_id=1, source_target_pairs={{0,6},{2,4},{4,2},{6,0},{8,14},{10,12},{12,10},{14,8},{1,7},{3,5},... | collective-permute-start | bytes 393224 | tf_op jit(solution)/shard_map/ppermute | solution.py:336
  10.1 1.3 %copy-start.3 = (bf16[2,2,192,192]{3,2,1,0:T(8,128)(2,1)}, bf16[2,2,192,192]{3,2,1,0:T(8,128)(2,1)S(1)}, u32[]{:S(2)}) copy-start(bf16[2,2,192,192]{3,2,1,0:T(8,128)(2,1)S(1)} %get-tuple-element.37.refs_5_) | copy-start | bytes 884740
  10.5 1.0 %copy-start.10 = (bf16[1,64]{1,0:T(2,128)(2,1)S(1)}, bf16[1,64]{1,0:T(2,128)(2,1)}, u32[]{:S(2)}) copy-start(bf16[1,64]{1,0:T(2,128)(2,1)} %row_ref.1) | copy-start | bytes 388
  11.4 1.7 %copy-start.5 = (f32[8,64,128]{2,1,0:T(8,128)S(1)}, f32[8,64,128]{2,1,0:T(8,128)}, u32[]{:S(2)}) copy-start(f32[8,64,128]{2,1,0:T(8,128)} %get-tuple-element.31.own_ref) | copy-start | bytes 786436
  11.4 1.7 %collective-permute-start.7 = (f32[64,256]{1,0:T(8,128)S(1)}, f32[64,256]{1,0:T(8,128)S(1)}, u32[]{:S(2)}, u32[]{:S(2)}) collective-permute-start(f32[64,256]{1,0:T(8,128)S(1)} %sums.1.after_ref.message_ref), channel_id=1, source_target_pairs={{0,1},{1,0},{2,3},{3,2},{4,5},{5,4},{6,7},{7,6},{8,9},{9,8},{10,11... | collective-permute-start | bytes 196616 | tf_op jit(solution)/shard_map/ppermute | solution.py:336
  13.2 10.7 %collective-permute-start.8 = (bf16[10,64,128]{2,1,0:T(8,128)(2,1)S(1)}, bf16[10,64,128]{2,1,0:T(8,128)(2,1)S(1)}, u32[]{:S(2)}, u32[]{:S(2)}) collective-permute-start(bf16[10,64,128]{2,1,0:T(8,128)(2,1)S(1)} %merge.1.sent_ref), channel_id=1, source_target_pairs={{0,8},{2,10},{4,12},{6,14},{8,0},{10,2},{12,4},{14,6},{1,9},{3,11}... | collective-permute-start | bytes 491528 | tf_op jit(solution)/shard_map/ppermute | solution.py:336
  16.0 7.3 %collective-permute-start.3 = (bf16[8,64,128]{2,1,0:T(8,128)(2,1)S(1)}, bf16[8,64,128]{2,1,0:T(8,128)(2,1)S(1)}, u32[]{:S(2)}, u32[]{:S(2)}) collective-permute-start(bf16[8,64,128]{2,1,0:T(8,128)(2,1)S(1)} %get-tuple-element.30), channel_id=1, source_target_pairs={{0,6},{2,4},{4,2},{6,0},{8,14},{10,12},{12,10},{14,8},{1,7},{3,5},... | collective-permute-start | bytes 393224 | tf_op jit(solution)/shard_map/ppermute | solution.py:336
  18.5 10.0 %collective-permute-start.1 = (bf16[8,64,128]{2,1,0:T(8,128)(2,1)S(1)}, bf16[8,64,128]{2,1,0:T(8,128)(2,1)S(1)}, u32[]{:S(2)}, u32[]{:S(2)}) collective-permute-start(bf16[8,64,128]{2,1,0:T(8,128)(2,1)S(1)} %get-tuple-element.28), channel_id=1, source_target_pairs={{0,2},{2,0},{4,6},{6,4},{8,10},{10,8},{12,14},{14,12},{1,3},{3,1},... | collective-permute-start | bytes 393224 | tf_op jit(solution)/shard_map/ppermute | solution.py:336
  19.1 9.4 %collective-permute-start.2 = (bf16[8,64,128]{2,1,0:T(8,128)(2,1)S(1)}, bf16[8,64,128]{2,1,0:T(8,128)(2,1)S(1)}, u32[]{:S(2)}, u32[]{:S(2)}) collective-permute-start(bf16[8,64,128]{2,1,0:T(8,128)(2,1)S(1)} %get-tuple-element.29), channel_id=1, source_target_pairs={{0,4},{2,6},{4,0},{6,2},{8,12},{10,14},{12,8},{14,10},{1,5},{3,7},... | collective-permute-start | bytes 393224 | tf_op jit(solution)/shard_map/ppermute | solution.py:336
  23.9 11.6 %collective-permute-start.9 = (bf16[10,64,128]{2,1,0:T(8,128)(2,1)S(1)}, bf16[10,64,128]{2,1,0:T(8,128)(2,1)S(1)}, u32[]{:S(2)}, u32[]{:S(2)}) collective-permute-start(bf16[10,64,128]{2,1,0:T(8,128)(2,1)S(1)} %get-tuple-element.34), channel_id=1, source_target_pairs={{0,6},{2,4},{4,2},{6,0},{8,14},{10,12},{12,10},{14,8},{1,7},{3,5},... | collective-permute-start | bytes 491528 | tf_op jit(solution)/shard_map/ppermute | solution.py:336
  26.8 12.3 %collective-permute-start.13 = (bf16[10,64,128]{2,1,0:T(8,128)(2,1)S(1)}, bf16[10,64,128]{2,1,0:T(8,128)(2,1)S(1)}, u32[]{:S(2)}, u32[]{:S(2)}) collective-permute-start(bf16[10,64,128]{2,1,0:T(8,128)(2,1)S(1)} %get-tuple-element.35.refs_0_), channel_id=1, source_target_pairs={{0,2},{2,0},{4,6},{6,4},{8,10},{10,8},{12,14},{14,12},{1,3},{3,1},... | collective-permute-start | bytes 491528 | tf_op jit(solution)/shard_map/ppermute | solution.py:336
  28.6 7.0 %collective-permute-start.4 = (bf16[8,64,128]{2,1,0:T(8,128)(2,1)S(1)}, bf16[8,64,128]{2,1,0:T(8,128)(2,1)S(1)}, u32[]{:S(2)}, u32[]{:S(2)}) collective-permute-start(bf16[8,64,128]{2,1,0:T(8,128)(2,1)S(1)} %add_convert_fusion.first_ref), channel_id=1, source_target_pairs={{0,8},{2,10},{4,12},{6,14},{8,0},{10,2},{12,4},{14,6},{1,9},{3,11}... | collective-permute-start | bytes 393224 | tf_op jit(solution)/shard_map/ppermute | solution.py:336
  29.8 9.9 %collective-permute-start.14 = (bf16[12,64,128]{2,1,0:T(8,128)(2,1)S(1)}, bf16[12,64,128]{2,1,0:T(8,128)(2,1)S(1)}, u32[]{:S(2)}, u32[]{:S(2)}) collective-permute-start(bf16[12,64,128]{2,1,0:T(8,128)(2,1)S(1)} %get-tuple-element.36), channel_id=1, source_target_pairs={{0,4},{2,6},{4,0},{6,2},{8,12},{10,14},{12,8},{14,10},{1,5},{3,7},... | collective-permute-start | bytes 589832 | tf_op jit(solution)/shard_map/ppermute | solution.py:336
  35.6 8.3 %collective-permute-start.12 = (bf16[8,64,128]{2,1,0:T(8,128)(2,1)S(1)}, bf16[8,64,128]{2,1,0:T(8,128)(2,1)S(1)}, u32[]{:S(2)}, u32[]{:S(2)}) collective-permute-start(bf16[8,64,128]{2,1,0:T(8,128)(2,1)S(1)} %add.30.refs_6_.refs_0_), channel_id=1, source_target_pairs={{0,6},{2,4},{4,2},{6,0},{8,14},{10,12},{12,10},{14,8},{1,7},{3,5},... | collective-permute-start | bytes 393224 | tf_op jit(solution)/shard_map/ppermute | solution.py:336
  37.8 6.6 %collective-permute-start.11 = (bf16[8,64,128]{2,1,0:T(8,128)(2,1)S(1)}, bf16[8,64,128]{2,1,0:T(8,128)(2,1)S(1)}, u32[]{:S(2)}, u32[]{:S(2)}) collective-permute-start(bf16[8,64,128]{2,1,0:T(8,128)(2,1)S(1)} %add.30.refs_6_.refs_0_), channel_id=1, source_target_pairs={{0,4},{2,6},{4,0},{6,2},{8,12},{10,14},{12,8},{14,10},{1,5},{3,7},... | collective-permute-start | bytes 393224 | tf_op jit(solution)/shard_map/ppermute | solution.py:336
  38.6 5.8 %collective-permute-start.10 = (bf16[8,64,128]{2,1,0:T(8,128)(2,1)S(1)}, bf16[8,64,128]{2,1,0:T(8,128)(2,1)S(1)}, u32[]{:S(2)}, u32[]{:S(2)}) collective-permute-start(bf16[8,64,128]{2,1,0:T(8,128)(2,1)S(1)} %add.30.refs_6_.refs_0_), channel_id=1, source_target_pairs={{0,2},{2,0},{4,6},{6,4},{8,10},{10,8},{12,14},{14,12},{1,3},{3,1},... | collective-permute-start | bytes 393224 | tf_op jit(solution)/shard_map/ppermute | solution.py:336
  39.1 1.0 %copy-start.4 = (bf16[2,2,192,192]{3,2,1,0:T(8,128)(2,1)S(1)}, bf16[2,2,192,192]{3,2,1,0:T(8,128)(2,1)}, u32[]{:S(2)}) copy-start(bf16[2,2,192,192]{3,2,1,0:T(8,128)(2,1)} %copy-done.3) | copy-start | bytes 884740
  39.8 1.3 %collective-permute-start.15 = (bf16[2,64,128]{2,1,0:T(8,128)(2,1)S(1)}, bf16[2,64,128]{2,1,0:T(8,128)(2,1)S(1)}, u32[]{:S(2)}, u32[]{:S(2)}) collective-permute-start(bf16[2,64,128]{2,1,0:T(8,128)(2,1)S(1)} %slice_select_fusion.1), channel_id=1, source_target_pairs={{0,1},{1,0},{2,3},{3,2},{4,5},{5,4},{6,7},{7,6},{8,9},{9,8},{10,11... | collective-permute-start | bytes 98312 | tf_op jit(solution)/shard_map/ppermute | solution.py:336
  40.1 1.0 %copy-start.6 = (bf16[128,64]{0,1:T(8,128)(2,1)S(1)}, bf16[128,64]{0,1:T(8,128)(2,1)}, u32[]{:S(2)}) copy-start(bf16[128,64]{0,1:T(8,128)(2,1)} %param.15) | copy-start | bytes 49156
  (3 other events, 2.2 us)
